TPU v7x, 128 devices: a whole 4x4x4 slice. The times are simulated.
128 devices in a mesh: rep: 16 (over z, y_lo, core), shard: 8 (over x, y_hi).
Axes of the slice: x: 4, y: 4 (y_hi: 2, y_lo: 2; y = y_hi * 2 + y_lo), z: 4, core: 2. Of those that a mesh axis runs over, the one named last changes fastest.
Arguments:
- tokens: bfloat16 [32768, 1024], P(('rep', 'shard')), may hold values from -24 to 24
- cotangent: bfloat16 [32768, 1024], P(('rep', 'shard')), may hold values from -6 to 6
- segment_ids: int32 [128, 256], P(('rep', 'shard')), may hold values from 0 to 2, as said below
- positions: int32 [128, 256], P(('rep', 'shard')), may hold values from 0 to 506, as said below
- master_qkv: float32 [1024, 4096], P('shard'), may hold values from -0.1875 to 0.1875
- master_out: float32 [2048, 1024], P('shard'), may hold values from -0.5 to 0.5
- master_gate_up: float32 [1024, 6144], P('shard'), may hold values from -0.1875 to 0.1875
- master_down: float32 [3072, 1024], P('shard'), may hold values from -0.109375 to 0.109375
- master_gains: float32 [2304], P('shard'), may hold values from 0.5 to 1.5
- first_qkv: float32 [1024, 4096], P('shard'), may hold values from -128 to 128
- first_out: float32 [2048, 1024], P('shard'), may hold values from -32 to 32
- first_gate_up: float32 [1024, 6144], P('shard'), may hold values from -48 to 48
- first_down: float32 [3072, 1024], P('shard'), may hold values from -64 to 64
- first_gains: float32 [2304], P('shard'), may hold values from -128 to 128
- second_qkv: float32 [1024, 4096], P('shard'), may hold values from 32.768 to 131.072
- second_out: float32 [2048, 1024], P('shard'), may hold values from 2.94912 to 11.79648
- second_gate_up: float32 [1024, 6144], P('shard'), may hold values from 5.24288 to 20.97152
- second_down: float32 [3072, 1024], P('shard'), may hold values from 11.79648 to 47.18592
- second_gains: float32 [2304], P('shard'), may hold values from 32.768 to 131.072
Outputs:
- activations: bfloat16 [32768, 1024], P(('rep', 'shard'))
- input_grad: bfloat16 [32768, 1024], P(('rep', 'shard'))
- new_master_qkv: float32 [1024, 4096], P('shard')
- new_master_out: float32 [2048, 1024], P('shard')
- new_master_gate_up: float32 [1024, 6144], P('shard')
- new_master_down: float32 [3072, 1024], P('shard')
- new_master_gains: float32 [2304], P('shard')
- new_first_qkv: float32 [1024, 4096], P('shard')
- new_first_out: float32 [2048, 1024], P('shard')
- new_first_gate_up: float32 [1024, 6144], P('shard')
- new_first_down: float32 [3072, 1024], P('shard')
- new_first_gains: float32 [2304], P('shard')
- new_second_qkv: float32 [1024, 4096], P('shard')
- new_second_out: float32 [2048, 1024], P('shard')
- new_second_gate_up: float32 [1024, 6144], P('shard')
- new_second_down: float32 [3072, 1024], P('shard')
- new_second_gains: float32 [2304], P('shard')
Inputs may be any that keep to these rules, and one draw needn't show every extreme that they name: `segment_ids`: each row holds 3 documents, numbered from 0 and never falling along the row, each of one token or more. Within each document positions are 0 at its first token and rise by 1 or 2 from one token to the next; in one sequence the first document holds 254 tokens and rises by 2 throughout.
All inputs are finite; a program needn't handle non-finite values.
Results may differ from a plain program's by a relative error of at most 0.024.
Values may be sent and summed in bfloat16 or wider, within the bound.
A program may use at most 320 MiB of HBM per device.

v0:
```python
import math

import jax
import jax.numpy as jnp
from jax import lax
from jax.sharding import PartitionSpec as P

D = 1024
HEADS = 16
KV_HEADS = 8
HD = 128
FF = 3072
STEP = 10
Q_WIDTH = 2048
KV_WIDTH = 1024


def normed_parts(values, gain):
    scale = lax.rsqrt(jnp.mean(values * values, axis=-1, keepdims=True) + 1e-06)
    unit = values * scale
    return (unit * gain, unit, scale)


def norm_back(upstream, gain, unit, scale):
    pushed = upstream * gain
    inner = jnp.mean(pushed * unit, axis=-1, keepdims=True)
    return scale * (pushed - unit * inner)


def turned(values):
    middle = values.shape[-1] // 2
    return jnp.concatenate([-values[..., middle:], values[..., :middle]], axis=-1)


def rotate(values, cosine, sine):
    return values * cosine + turned(values) * sine


def unrotate(upstream, cosine, sine):
    moved = upstream * sine
    middle = moved.shape[-1] // 2
    return upstream * cosine + jnp.concatenate([moved[..., middle:], -moved[..., :middle]], axis=-1)


def rope_tables(positions):
    freq = jnp.exp(jnp.arange(HD // 2).astype(jnp.float32) * (-2.0 * math.log(1000000.0) / HD))
    angle = positions.astype(jnp.float32)[..., None] * freq
    cosine = jnp.cos(angle)
    sine = jnp.sin(angle)
    return (jnp.concatenate([cosine, cosine], axis=-1), jnp.concatenate([sine, sine], axis=-1))


def attention_scores(rotated_q, rotated_k, allowed):
    raw = jnp.einsum("tkrd,skd->krts", rotated_q, rotated_k, preferred_element_type=jnp.float32)
    return jnp.where(allowed, raw * HD ** (-0.5), -1e30)


def regroup(gradient, shards, replicas):
    shaped = gradient.reshape((shards, replicas, -1) + gradient.shape[1:])
    return jnp.swapaxes(shaped, 0, 1).reshape(gradient.shape)


def adamw_step(master, first, second, gradient, rate, decay):
    first_new = 0.9 * first + 0.1 * gradient
    second_new = 0.999 * second + 0.001 * gradient * gradient
    direction = first_new / (1.0 - 0.9**STEP) / (jnp.sqrt(second_new / (1.0 - 0.999**STEP)) + 1e-08)
    return (master - rate * (direction + decay * master), first_new, second_new)


def per_device(
    tokens,
    cotangent,
    segment_ids,
    positions,
    master_qkv,
    master_out,
    master_gate_up,
    master_down,
    master_gains,
    first_qkv,
    first_out,
    first_gate_up,
    first_down,
    first_gains,
    second_qkv,
    second_out,
    second_gate_up,
    second_down,
    second_gains,
):
    w_qkv, w_out, w_gate_up, w_down, gains = (
        lax.all_gather(master_qkv.astype(jnp.bfloat16), "shard", axis=0, tiled=True),
        lax.all_gather(master_out.astype(jnp.bfloat16), "shard", axis=0, tiled=True),
        lax.all_gather(master_gate_up.astype(jnp.bfloat16), "shard", axis=0, tiled=True),
        lax.all_gather(master_down.astype(jnp.bfloat16), "shard", axis=0, tiled=True),
        lax.all_gather(master_gains.astype(jnp.bfloat16), "shard", axis=0, tiled=True),
    )
    gain_all = gains.astype(jnp.float32)
    gain_in = gain_all[:D]
    gain_mid = gain_all[D : 2 * D]
    gain_query = gain_all[2 * D : 2 * D + HD]
    gain_key = gain_all[2 * D + HD :]
    length = tokens.shape[0]
    share = HEADS // KV_HEADS
    inputs = tokens.astype(jnp.float32)
    normal_in, unit_in, scale_in = normed_parts(inputs, gain_in)
    hidden_in = normal_in.astype(jnp.bfloat16)
    project = jnp.dot(hidden_in, w_qkv, preferred_element_type=jnp.float32)
    queries = project[:, :Q_WIDTH].reshape(length, KV_HEADS, share, HD)
    keys_raw = project[:, Q_WIDTH : Q_WIDTH + KV_WIDTH].reshape(length, KV_HEADS, HD)
    values = project[:, Q_WIDTH + KV_WIDTH :].reshape(length, KV_HEADS, HD).astype(jnp.bfloat16)
    cosine, sine = rope_tables(positions[0])
    cos_query = cosine[:, None, None, :]
    sin_query = sine[:, None, None, :]
    cos_key = cosine[:, None, :]
    sin_key = sine[:, None, :]
    normal_q, unit_q, scale_q = normed_parts(queries, gain_query)
    rotated_q = rotate(normal_q, cos_query, sin_query).astype(jnp.bfloat16)
    normal_k, unit_k, scale_k = normed_parts(keys_raw, gain_key)
    rotated_k = rotate(normal_k, cos_key, sin_key).astype(jnp.bfloat16)
    segments = segment_ids[0]
    places = jnp.arange(length)
    allowed = ((places[None, :] <= places[:, None]) & (segments[:, None] == segments[None, :]))[
        None, None
    ]
    scores = attention_scores(rotated_q, rotated_k, allowed)
    top = jnp.max(scores, axis=-1, keepdims=True)
    expo = jnp.exp(scores - top)
    total = jnp.sum(expo, axis=-1, keepdims=True)
    probs = (expo / total).astype(jnp.bfloat16)
    log_total = top + jnp.log(total)
    mixed = jnp.einsum("krts,skd->tkrd", probs, values, preferred_element_type=jnp.float32)
    mixed = mixed.reshape(length, Q_WIDTH).astype(jnp.bfloat16)
    middle = inputs + jnp.dot(mixed, w_out, preferred_element_type=jnp.float32)
    normal_mid, unit_mid, scale_mid = normed_parts(middle, gain_mid)
    hidden_mid = normal_mid.astype(jnp.bfloat16)
    gate_up = jnp.dot(hidden_mid, w_gate_up, preferred_element_type=jnp.float32)
    gate = gate_up[:, :FF]
    upward = gate_up[:, FF:]
    sigma = jax.nn.sigmoid(gate)
    swish = gate * sigma
    active = (swish * upward).astype(jnp.bfloat16)
    activations = (middle + jnp.dot(active, w_down, preferred_element_type=jnp.float32)).astype(
        jnp.bfloat16
    )
    grad_down = jnp.dot(active.T, cotangent, preferred_element_type=jnp.float32)
    pulled = jnp.dot(cotangent, w_down.T, preferred_element_type=jnp.float32)
    grad_gate = pulled * upward * sigma * (1.0 + gate * (1.0 - sigma))
    grad_upward = pulled * swish
    back_gate_up = jnp.concatenate([grad_gate, grad_upward], axis=-1).astype(jnp.bfloat16)
    grad_gate_up = jnp.dot(hidden_mid.T, back_gate_up, preferred_element_type=jnp.float32)
    back_mid = jnp.dot(back_gate_up, w_gate_up.T, preferred_element_type=jnp.float32)
    gain_grad_mid = jnp.sum(back_mid * unit_mid, axis=0)
    back_middle = cotangent.astype(jnp.float32) + norm_back(back_mid, gain_mid, unit_mid, scale_mid)
    back_branch = back_middle.astype(jnp.bfloat16)
    grad_out = jnp.dot(mixed.T, back_branch, preferred_element_type=jnp.float32)
    back_mixed = jnp.dot(back_branch, w_out.T, preferred_element_type=jnp.float32).astype(
        jnp.bfloat16
    )
    back_mixed = back_mixed.reshape(length, KV_HEADS, share, HD)
    scores_again = attention_scores(rotated_q, rotated_k, allowed)
    probs_again = jnp.exp(scores_again - log_total)
    back_probs = jnp.einsum(
        "tkrd,skd->krts", back_mixed, values, preferred_element_type=jnp.float32
    )
    inner = jnp.sum(probs_again * back_probs, axis=-1, keepdims=True)
    back_scores = (probs_again * (back_probs - inner) * HD ** (-0.5)).astype(jnp.bfloat16)
    back_query = jnp.einsum(
        "krts,skd->tkrd", back_scores, rotated_k, preferred_element_type=jnp.float32
    )
    back_key = jnp.einsum(
        "krts,tkrd->skd", back_scores, rotated_q, preferred_element_type=jnp.float32
    )
    back_value = jnp.einsum(
        "krts,tkrd->skd",
        probs_again.astype(jnp.bfloat16),
        back_mixed,
        preferred_element_type=jnp.float32,
    )
    plain_query = unrotate(back_query, cos_query, sin_query)
    gain_grad_query = jnp.sum(plain_query * unit_q, axis=(0, 1, 2))
    raw_query = norm_back(plain_query, gain_query, unit_q, scale_q)
    plain_key = unrotate(back_key, cos_key, sin_key)
    gain_grad_key = jnp.sum(plain_key * unit_k, axis=(0, 1))
    raw_key = norm_back(plain_key, gain_key, unit_k, scale_k)
    back_project = jnp.concatenate(
        [
            raw_query.reshape(length, Q_WIDTH),
            raw_key.reshape(length, KV_WIDTH),
            back_value.reshape(length, KV_WIDTH),
        ],
        axis=-1,
    ).astype(jnp.bfloat16)
    grad_qkv = jnp.dot(hidden_in.T, back_project, preferred_element_type=jnp.float32)
    back_in = jnp.dot(back_project, w_qkv.T, preferred_element_type=jnp.float32)
    gain_grad_in = jnp.sum(back_in * unit_in, axis=0)
    input_grad = (back_middle + norm_back(back_in, gain_in, unit_in, scale_in)).astype(jnp.bfloat16)
    grad_gains = jnp.concatenate([gain_grad_in, gain_grad_mid, gain_grad_query, gain_grad_key])
    shards = lax.axis_size("shard")
    replicas = lax.axis_size("rep")
    pieces = (
        lax.psum_scatter(
            regroup(grad_qkv, shards, replicas), ("rep", "shard"), scatter_dimension=0, tiled=True
        ),
        lax.psum_scatter(
            regroup(grad_out, shards, replicas), ("rep", "shard"), scatter_dimension=0, tiled=True
        ),
        lax.psum_scatter(
            regroup(grad_gate_up, shards, replicas),
            ("rep", "shard"),
            scatter_dimension=0,
            tiled=True,
        ),
        lax.psum_scatter(
            regroup(grad_down, shards, replicas), ("rep", "shard"), scatter_dimension=0, tiled=True
        ),
        lax.psum_scatter(
            regroup(grad_gains, shards, replicas), ("rep", "shard"), scatter_dimension=0, tiled=True
        ),
    )
    summed = (
        lax.all_gather(pieces[0].astype(jnp.bfloat16), "rep", axis=0, tiled=True).astype(
            jnp.float32
        ),
        lax.all_gather(pieces[1].astype(jnp.bfloat16), "rep", axis=0, tiled=True).astype(
            jnp.float32
        ),
        lax.all_gather(pieces[2].astype(jnp.bfloat16), "rep", axis=0, tiled=True).astype(
            jnp.float32
        ),
        lax.all_gather(pieces[3].astype(jnp.bfloat16), "rep", axis=0, tiled=True).astype(
            jnp.float32
        ),
        lax.all_gather(pieces[4].astype(jnp.bfloat16), "rep", axis=0, tiled=True).astype(
            jnp.float32
        ),
    )
    masters = (master_qkv, master_out, master_gate_up, master_down, master_gains)
    firsts = (first_qkv, first_out, first_gate_up, first_down, first_gains)
    seconds = (second_qkv, second_out, second_gate_up, second_down, second_gains)
    rates = (0.05, 0.05, 0.05, 0.05, 0.4)
    decays = (0.1, 0.1, 0.1, 0.1, 0.0)
    updated = [
        adamw_step(
            masters[index],
            firsts[index],
            seconds[index],
            summed[index],
            rates[index],
            decays[index],
        )
        for index in range(5)
    ]
    return (
        activations,
        input_grad,
        updated[0][0],
        updated[1][0],
        updated[2][0],
        updated[3][0],
        updated[4][0],
        updated[0][1],
        updated[1][1],
        updated[2][1],
        updated[3][1],
        updated[4][1],
        updated[0][2],
        updated[1][2],
        updated[2][2],
        updated[3][2],
        updated[4][2],
    )


def solution(mesh):
    in_specs = (
        P(("rep", "shard"), None),
        P(("rep", "shard"), None),
        P(("rep", "shard"), None),
        P(("rep", "shard"), None),
        P("shard", None),
        P("shard", None),
        P("shard", None),
        P("shard", None),
        P("shard"),
        P("shard", None),
        P("shard", None),
        P("shard", None),
        P("shard", None),
        P("shard"),
        P("shard", None),
        P("shard", None),
        P("shard", None),
        P("shard", None),
        P("shard"),
    )
    out_specs = (
        P(("rep", "shard"), None),
        P(("rep", "shard"), None),
        P("shard", None),
        P("shard", None),
        P("shard", None),
        P("shard", None),
        P("shard"),
        P("shard", None),
        P("shard", None),
        P("shard", None),
        P("shard", None),
        P("shard"),
        P("shard", None),
        P("shard", None),
        P("shard", None),
        P("shard", None),
        P("shard"),
    )
    return jax.shard_map(
        per_device, mesh=mesh, in_specs=in_specs, out_specs=out_specs, check_vma=False
    )
```

profile of v0, /device:TPU:1, one launch (start us, length us, event | category | flops | bytes accessed | tf_op | source)
XLA Modules:
  0.0 3296.9 jit_solution(15261528874588677301)
XLA Ops:
  17.9 22.0 all-reduce
  40.6 83.1 %all-gather.7.cloned.1.call-done = bf16[1024,4096]{1,0:T(8,128)(2,1)} async-done(((bf16[128,4096]{1,0:T(8,128)(2,1)}), bf16[1024,4096]{1,0:T(8,128)(2,1)}) %all-gather.7.cloned.1.call-update) | async-done | bytes 8388624 | tf_op jit(solution)/shard_map/all_gather | solution.py:92
  123.7 5.8 fusion.61
  140.0 4.9 multiply_reduce_fusion.2
  154.5 41.5 %all-gather.9.cloned.1.call-done = bf16[2048,1024]{1,0:T(8,128)(2,1)} async-done(((bf16[256,1024]{1,0:T(8,128)(2,1)}), bf16[2048,1024]{1,0:T(8,128)(2,1)}) %all-gather.9.cloned.1.call-update) | async-done | bytes 4194320 | tf_op jit(solution)/shard_map/all_gather | solution.py:93
  196.1 4.9 multiply_reduce_fusion.7
  201.0 143.4 %all-gather.11.cloned.1.call-done = bf16[1024,6144]{1,0:T(8,128)(2,1)} async-done(((bf16[128,6144]{1,0:T(8,128)(2,1)}), bf16[1024,6144]{1,0:T(8,128)(2,1)}) %all-gather.11.cloned.1.call-update) | async-done | bytes 12582928 | tf_op jit(solution)/shard_map/all_gather | solution.py:94
  344.3 11.2 fusion.73
  355.5 79.1 %all-gather.13.cloned.1.call-done = bf16[3072,1024]{1,0:T(8,128)(2,1)} async-done(((bf16[384,1024]{1,0:T(8,128)(2,1)}), bf16[3072,1024]{1,0:T(8,128)(2,1)}) %all-gather.13.cloned.1.call-update) | async-done | bytes 6291472 | tf_op jit(solution)/shard_map/all_gather | solution.py:95
  434.6 9.8 multiply_convert_fusion.1
  444.5 10.4 multiply_reduce_fusion.4
  470.0 9.4 broadcast_multiply_fusion
  479.4 10.0 bitcast_multiply_fusion.1
  499.5 6.2 copy.143
  507.4 11.7 fusion.20
  519.2 17.5 copy.145
  544.7 7.7 fusion.89
  552.4 11.9 copy.146
  566.2 612.7 %reduce-scatter.5.cloned.1.call-done = f32[8,4096]{1,0:T(8,128)} async-done(((f32[1024,4096]{1,0:T(8,128)}), f32[8,4096]{1,0:T(8,128)}) %reduce-scatter.5.cloned.1.call-update) | async-done | bytes 131088 | tf_op jit(solution)/shard_map/reduce_scatter | solution.py:202
  1180.5 7.3 fusion.44
  1188.1 99.7 %all-reduce.2 = bf16[2304]{0:T(1024)(128)(2,1)S(1)} all-reduce(f32[2304]{0:T(1024)S(1)} %reshape.224), channel_id=6, replica_groups=mesh['rep'=16,'shard'=8] {'rep','shard'}, use_global_device_ids=true, to_apply=%region_19.20.clone | all-reduce | flops 2304 | bytes 13824
  1288.0 30.0 all-reduce.1
  1320.5 5.5 fusion.33
  1326.0 569.5 %reduce-scatter.9.cloned.1.call-done = f32[8,6144]{1,0:T(8,128)} async-done(((f32[1024,6144]{1,0:T(8,128)}), f32[8,6144]{1,0:T(8,128)}) %reduce-scatter.9.cloned.1.call-update) | async-done | bytes 196624 | tf_op jit(solution)/shard_map/reduce_scatter | solution.py:208
  1897.7 646.7 %reduce-scatter.7.cloned.1.call-done = f32[16,1024]{1,0:T(8,128)} async-done(((f32[2048,1024]{1,0:T(8,128)}), f32[16,1024]{1,0:T(8,128)}) %reduce-scatter.7.cloned.1.call-update) | async-done | bytes 65552 | tf_op jit(solution)/shard_map/reduce_scatter | solution.py:205
  2545.3 33.4 %all_gather.36 = bf16[256,1024]{1,0:T(8,128)(2,1)S(1)} all-gather(bf16[16,1024]{1,0:T(8,128)(2,1)S(1)} %convert_element_type.151), channel_id=1, replica_groups=mesh['rep'=16,'shard'=8] {'rep'}, dimensions={0}, use_global_device_ids=true | all-gather | bytes 557056 | tf_op jit(solution)/shard_map/all_gather | solution.py:225
  2582.6 624.7 %reduce-scatter.11.cloned.1.call-done = f32[24,1024]{1,0:T(8,128)} async-done(((f32[3072,1024]{1,0:T(8,128)}), f32[24,1024]{1,0:T(8,128)}) %reduce-scatter.11.cloned.1.call-update) | async-done | bytes 98320 | tf_op jit(solution)/shard_map/reduce_scatter | solution.py:214
  3208.2 32.1 all_gather.38
  3240.3 5.0 multiply_subtract_fusion.2
  3247.9 7.0 multiply_subtract_fusion.1
  3254.9 28.4 all-gather.17.cloned.1.call-done
  3283.3 6.5 multiply_subtract_fusion
  (173 shorter events, 81.8 us)
Async XLA Ops:
  7.2 5.1 copy-start.2
  7.2 116.5 %all-gather.7.cloned.1.call-start = ((), (), s32[]{:S(2)}) async-start(), calls=%async_computation.4 | async-start | bytes 9437184 | tf_op jit(solution)/shard_map/all_gather | solution.py:92
  10.1 186.0 %all-gather.9.cloned.1.call-start = ((), (), s32[]{:S(2)}) async-start(), calls=%async_computation.5 | async-start | bytes 4718592 | tf_op jit(solution)/shard_map/all_gather | solution.py:93
  12.3 332.0 %all-gather.11.cloned.1.call-start = ((), (), s32[]{:S(2)}) async-start(), calls=%async_computation.6 | async-start | bytes 14155776 | tf_op jit(solution)/shard_map/all_gather | solution.py:94
  13.7 2.7 copy-start.35
  13.7 2.7 copy-start.37
  13.7 26.6 copy-start.10
  13.7 26.8 copy-start.32
  13.7 420.9 %all-gather.13.cloned.1.call-start = ((), (), s32[]{:S(2)}) async-start(), calls=%async_computation.7 | async-start | bytes 7077888 | tf_op jit(solution)/shard_map/all_gather | solution.py:95
  16.3 1162.5 %reduce-scatter.5.cloned.1.call-start = ((), (), s32[]{:S(2)}) async-start(), calls=%async_computation.8 | async-start | bytes 16908288 | tf_op jit(solution)/shard_map/reduce_scatter | solution.py:202
  147.9 3.4 copy-start.26
  434.6 9.8 copy-start.4
  444.5 10.4 copy-start.28
  444.5 10.4 copy-start.21
  464.1 4.2 copy-start.1
  464.1 4.2 copy-start.8
  489.3 3.1 copy-start.20
  495.6 4.0 copy-start.23
  496.2 3.4 copy-start.15
  505.7 1389.8 %reduce-scatter.9.cloned.1.call-start = ((), (), s32[]{:S(2)}) async-start(), calls=%async_computation.11 | async-start | bytes 25362432 | tf_op jit(solution)/shard_map/reduce_scatter | solution.py:208
  536.7 2007.7 %reduce-scatter.7.cloned.1.call-start = ((), (), s32[]{:S(2)}) async-start(), calls=%async_computation.10 | async-start | bytes 8454144 | tf_op jit(solution)/shard_map/reduce_scatter | solution.py:205
  543.6 2663.6 %reduce-scatter.11.cloned.1.call-start = ((), (), s32[]{:S(2)}) async-start(), calls=%async_computation.13 | async-start | bytes 12681216 | tf_op jit(solution)/shard_map/reduce_scatter | solution.py:214
  564.3 616.2 %copy-start.12 = (bf16[256,1024]{1,0:T(8,128)(2,1)S(1)}, bf16[256,1024]{1,0:T(8,128)(2,1)}, u32[]{:S(2)}) copy-start(bf16[256,1024]{1,0:T(8,128)(2,1)} %param.19) | copy-start | bytes 1572868
  564.3 616.2 %copy-start.24 = (bf16[256,8,128]{0,2,1:T(8,128)(2,1)S(1)}, bf16[256,8,128]{0,2,1:T(8,128)(2,1)}, u32[]{:S(2)}) copy-start(bf16[256,8,128]{0,2,1:T(8,128)(2,1)} %copy-done.23) | copy-start | bytes 1572868
  564.3 2683.6 %all-gather.15.cloned.1.call-start = ((), (), s32[]{:S(2)}) async-start(), calls=%async_computation.9 | async-start | bytes 1114112 | tf_op jit(solution)/shard_map/all_gather | solution.py:222
  1180.4 2102.9 %all-gather.17.cloned.1.call-start = ((), (), s32[]{:S(2)}) async-start(), calls=%async_computation.12 | async-start | bytes 1671168 | tf_op jit(solution)/shard_map/all_gather | solution.py:228
  1320.5 576.6 %copy-start.31 = (f32[288]{0:T(512)S(1)}, f32[288]{0:T(512)}, u32[]{:S(2)}) copy-start(f32[288]{0:T(512)} %param.27) | copy-start | bytes 3460
  1320.5 576.6 %copy-start.33 = (f32[288]{0:T(512)S(1)}, f32[288]{0:T(512)}, u32[]{:S(2)}) copy-start(f32[288]{0:T(512)} %param.32) | copy-start | bytes 3460
  1320.5 576.6 %copy-start.34 = (f32[288]{0:T(512)S(1)}, f32[288]{0:T(512)}, u32[]{:S(2)}) copy-start(f32[288]{0:T(512)} %param.37) | copy-start | bytes 3460
  1320.5 1258.2 %copy-start.13 = (f32[256,1024]{1,0:T(8,128)S(1)}, f32[256,1024]{1,0:T(8,128)}, u32[]{:S(2)}) copy-start(f32[256,1024]{1,0:T(8,128)} %param.24) | copy-start | bytes 3145732
  2578.7 661.6 %copy-start.9 = (f32[384,1024]{1,0:T(8,128)S(1)}, f32[384,1024]{1,0:T(8,128)}, u32[]{:S(2)}) copy-start(f32[384,1024]{1,0:T(8,128)} %param.26) | copy-start | bytes 4718596
  3245.3 38.0 %copy-start.3 = (f32[128,6144]{1,0:T(8,128)S(1)}, f32[128,6144]{1,0:T(8,128)}, u32[]{:S(2)}) copy-start(f32[128,6144]{1,0:T(8,128)} %param.25) | copy-start | bytes 9437188
  (16 other events, 25.0 us)
Sparse Core Ops, SparseCore 0:
  10.9 112.7 all-gather.6
  126.6 69.4 all-gather.8
  199.0 145.3 all-gather.10
  347.1 87.5 all-gather.12
  505.9 672.9 reduce-scatter.4
  1181.1 714.3 reduce-scatter.8
  1897.9 646.5 reduce-scatter.6
  2547.0 660.2 reduce-scatter.10
  3209.5 38.3 all-gather.14
  3250.0 33.2 all-gather.16
where the time goes:
time: 3300 us
  waiting for transfers between devices  2830 us (86%)
  blocking collectives  217 us (7%)
  matrix products  111 us (3%)
  local copies, waits for them, and re-layouts  66.4 us (2%)
  other arithmetic  54.3 us (2%)
    reduce_scatter x1, waiting for transfers between devices, per_device(): lax.psum_scatter(regroup(grad_out, shards, replicas), ('rep', 'shard'), s...  647 us
    reduce_scatter x1, waiting for transfers between devices, per_device(): lax.psum_scatter(regroup(grad_down, shards, replicas), ('rep', 'shard'),...  625 us
    reduce_scatter x1, waiting for transfers between devices, per_device(): lax.psum_scatter(regroup(grad_qkv, shards, replicas), ('rep', 'shard'), s...  613 us
    reduce_scatter x1, waiting for transfers between devices, per_device(): lax.psum_scatter(regroup(grad_gate_up, shards, replicas), ('rep', 'shard'...  569 us
    unnamed x3, blocking collectives  152 us
    all_gather x1, waiting for transfers between devices, per_device(): lax.all_gather(master_gate_up.astype(jnp.bfloat16), 'shard', axis=0, tile...  143 us
    all_gather x1, waiting for transfers between devices, per_device(): lax.all_gather(master_qkv.astype(jnp.bfloat16), 'shard', axis=0, tiled=True)  83.1 us
    all_gather x1, waiting for transfers between devices, per_device(): lax.all_gather(master_down.astype(jnp.bfloat16), 'shard', axis=0, tiled=T...  79.1 us
  transfers between devices with their start and end apart: 10, of which 10 were waited for; matrix products, arithmetic and copies ran while one was open for 4% of the time, Pallas kernels for 0%

commit v1 on v0

v1 whole, which is shorter than its diff:
```python
import math

import jax
import jax.numpy as jnp
from jax import lax
from jax.experimental import pallas as pl
from jax.experimental.pallas import tpu as pltpu
from jax.sharding import PartitionSpec as P

D = 1024
HEADS = 16
KV_HEADS = 8
HD = 128
FF = 3072
STEP = 10
Q_WIDTH = 2048
KV_WIDTH = 1024
TOK = 256
F32 = jnp.float32
BF16 = jnp.bfloat16
EPS = 1e-06
SCALE = HD ** (-0.5)

QKV0, OUT0, GAIN0, GU0, DN0, WCOLS = 0, 2048, 3072, 3200, 6272, 7808
G_OUT, G_GAIN, G_DN, G_COLS = 0, 1024, 1152, 2688
S_QKV, S_GU = 2688, 4736
ROTATIONS = (("x", "y", "z"), ("y", "z", "x"), ("z", "x", "y"))


def dot(left, right):
    return jnp.dot(left, right, preferred_element_type=F32)


def dot_nt(left, right):
    return lax.dot_general(left, right, (((1,), (1,)), ((), ())), preferred_element_type=F32)


def dot_tn(left, right):
    return lax.dot_general(left, right, (((0,), (0,)), ((), ())), preferred_element_type=F32)


def lanes(start, size, step=128):
    return pl.ds(start if isinstance(start, int) else pl.multiple_of(start, step), size)


def coordinates():
    rep = lax.axis_index("rep")
    shard = lax.axis_index("shard")
    return {
        "x": shard // 2,
        "y": (shard % 2) * 2 + (rep // 2) % 2,
        "z": rep // 4,
        "c": rep % 2,
    }


def device(at):
    return {"rep": at["z"] * 4 + (at["y"] % 2) * 2 + at["c"], "shard": at["x"] * 2 + at["y"] // 2}


def moved(me, axis, by):
    return {**me, axis: (me[axis] + by + 4) % 4}


def view(ref, select, offset, size):
    where = tuple(select.get(axis, slice(None)) for axis in "xyz")
    return ref.at[where + (slice(None), lanes(offset, size))]


def layer_kernel(
    tokens,
    cotangent,
    tables,
    bias,
    piece,
    activations,
    input_grad,
    summed,
    weights,
    grads,
    other_weights,
    got_far,
    got_near,
    got_two,
    got_three,
    toks,
    cots,
    rope,
    mask,
    hidden,
    raw,
    rotated,
    vals,
    mixed,
    part,
    got_part,
    got_down,
    middle,
    hidden_mid,
    gate_up,
    active,
    branch,
    turned_lhs,
    out_low,
    gains_acc,
    local_sem,
    send_sem,
    recv_sem,
):
    me = coordinates()
    c = me["c"]
    sib = 1 - c
    x, y, z = me["x"], me["y"], me["z"]
    sibling = device({**me, "c": sib})
    used = [0]

    class Transfer:
        def __init__(self, source, there, here, target):
            self.index = used[0]
            used[0] += 1
            self.source, self.there, self.here, self.target = source, there, here, target
            self.copy(source, there).start()

        def copy(self, source, there):
            return pltpu.make_async_remote_copy(
                src_ref=source,
                dst_ref=there,
                send_sem=send_sem.at[self.index],
                recv_sem=recv_sem.at[self.index],
                device_id=self.target,
                device_id_type=pl.DeviceIdType.MESH,
            )

        def arrived(self):
            self.copy(self.here, self.here).wait_recv()

        def sent(self):
            self.copy(self.source, self.there).wait_send()

    pending = []

    def send(source, there, here, target):
        transfer = Transfer(source, there, here, target)
        pending.append(transfer)
        return transfer

    def flush():
        while pending:
            pending.pop(0).sent()

    def arrive(transfers):
        for transfer in transfers:
            transfer.arrived()

    own = view(weights, {"x": x, "y": y, "z": z}, 0, WCOLS)
    inward = [
        (tokens, toks.at[c]),
        (cotangent, cots.at[c]),
        (tables, rope.at[c]),
        (bias, mask.at[c]),
        (piece, own),
    ]
    for index, (source, target) in enumerate(inward):
        pltpu.make_async_copy(source, target, local_sem.at[index]).start()

    barrier = pltpu.get_barrier_semaphore()
    friends = [sibling] + [device(moved(me, axis, by)) for axis in "xyz" for by in (1, 2, 3)]
    for friend in friends:
        pl.semaphore_signal(barrier, inc=1, device_id=friend, device_id_type=pl.DeviceIdType.MESH)
    for index, (source, target) in enumerate(inward):
        pltpu.make_async_copy(source, target, local_sem.at[index]).wait()
    pl.semaphore_wait(barrier, len(friends))

    def gather_one(rotation, offset, size):
        first, second, third = rotation
        source = view(weights, {"x": x, "y": y, "z": z}, offset, size)
        out = []
        for by in (1, 2, 3):
            here = view(weights, {**{"x": x, "y": y, "z": z}, third: (me[third] - by + 4) % 4}, offset, size)
            out.append(send(source, source, here, device(moved(me, third, by))))
        return out

    def gather_two(rotation, offset, size):
        first, second, third = rotation
        source = view(weights, {first: me[first], second: me[second]}, offset, size)
        out = []
        for by in (1, 2, 3):
            here = view(weights, {first: me[first], second: (me[second] - by + 4) % 4}, offset, size)
            out.append(send(source, source, here, device(moved(me, second, by))))
        return out

    def gather_three(rotation, offset, size):
        first = rotation[0]
        source = view(weights, {first: me[first]}, offset, size)
        out = []
        for by in (1, 3):
            here = view(weights, {first: (me[first] - by + 4) % 4}, offset, size)
            out.append(send(source, source, here, device(moved(me, first, by))))
        return out

    def gather_four(rotation, offset, size):
        first, second = rotation[0], rotation[1]
        out = []
        for by, half in ((1, 0), (3, 1)):
            rows = pl.ds(2 * half, 2)
            source = view(weights, {first: (me[first] - by + 4) % 4, second: rows}, offset, size)
            here = view(weights, {first: (me[first] + 2) % 4, second: rows}, offset, size)
            out.append(send(source, source, here, device(moved(me, first, by))))
        return out

    chunks = (((0, 1024), (1024, 1024), (2048, 1152)), ((GU0, 1536), (GU0 + 1536, 1536), (DN0, 1536)))
    steps = (gather_one, gather_two, gather_three, gather_four)
    flying = [[None] * 3 for _ in chunks]

    def pump(chunk, step):
        for index, rotation in enumerate(ROTATIONS):
            if step:
                arrive(flying[chunk][index])
            if step < 4:
                flying[chunk][index] = steps[step](rotation, *chunks[chunk][index])

    pump(0, 0)
    early = [
        send(toks.at[c], toks.at[c], toks.at[sib], sibling),
        send(rope.at[c], rope.at[c], rope.at[sib], sibling),
        send(mask.at[c], mask.at[c], mask.at[sib], sibling),
        send(cots.at[c], cots.at[c], cots.at[sib], sibling),
    ]
    pump(1, 0)
    pump(0, 1)
    pump(1, 1)
    pump(0, 2)
    pump(1, 2)
    arrive(early)
    pump(0, 3)
    pump(0, 4)

    def to_other(offset, size, at):
        return send(
            view(weights, {"x": pl.ds(2 * sib, 2)}, offset, size),
            view(other_weights, {}, at, size),
            view(other_weights, {}, at, size),
            sibling,
        )

    other_out = to_other(OUT0, 1024, 0)

    def weight(offset, size):
        return weights[:, :, :, :, lanes(offset, size)].reshape(1024, size)

    def weight_rows(row, offset, size):
        return weights[row, :, :, :, lanes(offset, size)].reshape(256, size)

    def weight_own(offset, size):
        return weights[pl.ds(2 * c, 2), :, :, :, lanes(offset, size)].reshape(512, size)

    def weight_other(offset, size):
        return other_weights[:, :, :, :, lanes(offset, size)].reshape(512, size)

    gain_rows = jnp.zeros((16, 128), F32)
    head_rows = jnp.zeros((16, 128), F32)
    for part_x in range(4):
        for part_y in (0, 2):
            gain_rows += weights[part_x, part_y, 0, :, pl.ds(GAIN0, 128)].astype(F32)
            head_rows += weights[part_x, part_y, 1, :, pl.ds(GAIN0, 128)].astype(F32)
    gain_in = jnp.concatenate([gain_rows[i : i + 1] for i in range(8)], axis=1)
    gain_mid = jnp.concatenate([gain_rows[i : i + 1] for i in range(8, 16)], axis=1)
    gain_query = head_rows[0:1]
    gain_key = head_rows[1:2]

    def unit_of(values):
        scale = lax.rsqrt(jnp.mean(values * values, axis=-1, keepdims=True) + EPS)
        return values * scale, scale

    def norm_back(upstream, gain, unit, scale):
        pushed = upstream * gain
        inner = jnp.mean(pushed * unit, axis=-1, keepdims=True)
        return scale * (pushed - unit * inner)

    for b in range(2):
        unit, _ = unit_of(toks[b].astype(F32))
        hidden[b] = (unit * gain_in).astype(BF16)

    def all_hidden():
        return hidden[...].reshape(512, 1024)

    def project_heads(t, carry):
        values = dot(all_hidden(), weight(QKV0 + t * 256, 256))
        raw[:, lanes(t * 256, 256)] = values.astype(BF16)
        gain = jnp.where(t < 4, gain_query, gain_key)
        cosine = rope[:, :, 0:128].reshape(512, 128)
        sine = rope[:, :, 128:256].reshape(512, 128)
        for h in range(2):
            unit, _ = unit_of(values[:, h * 128 : (h + 1) * 128])
            normal = unit * gain
            rotated[2 * t + h] = (normal * cosine + pltpu.roll(normal, 64, 1) * sine).astype(BF16)
        return carry

    lax.fori_loop(0, 6, project_heads, 0)

    def project_values(t, carry):
        values = dot(all_hidden(), weight(QKV0 + 1536 + t * 256, 256)).astype(BF16)
        vals[2 * t] = values[:, :128]
        vals[2 * t + 1] = values[:, 128:]
        return carry

    lax.fori_loop(0, 2, project_values, 0)

    def probabilities(b, g):
        rows = pl.ds(pl.multiple_of(b * 256, 256), 256)
        query = rotated[pl.ds(2 * g, 2), rows, :].reshape(512, 128)
        key = rotated[8 + g, rows, :]
        scores = dot_nt(query, key).reshape(2, 256, 256) * SCALE + mask[b][None]
        scores = scores.reshape(512, 256)
        expo = jnp.exp(scores - jnp.max(scores, axis=-1, keepdims=True))
        probs = expo / jnp.sum(expo, axis=-1, keepdims=True)
        return rows, query, key, vals[g, rows, :], probs

    def attend(step, carry):
        b, g = step // 4, step % 4
        rows, query, key, value, probs = probabilities(b, g)
        result = dot(probs.astype(BF16), value).astype(BF16)
        for h in range(2):
            mixed[h, rows, lanes(g * 128, 128)] = result[h * 256 : (h + 1) * 256]
        return carry

    lax.fori_loop(0, 8, attend, 0)

    pump(1, 3)
    arrive([other_out])

    def two_parts(values, columns):
        part[0, :, columns] = values[:256]
        part[1, :, columns] = values[256:]

    def project_out(t, carry):
        values = dot(mixed[c], weight_own(OUT0 + t * 256, 256)) + dot(
            mixed[sib], weight_other(t * 256, 256)
        )
        two_parts(values, lanes(t * 256, 256))
        return carry

    lax.fori_loop(0, 4, project_out, 0)
    across = send(part.at[sib], got_part, got_part, sibling)
    across.arrived()
    middle[...] = toks[c].astype(F32) + part[c] + got_part[...]
    unit_mid, _ = unit_of(middle[...])
    hidden_mid[c] = (unit_mid * gain_mid).astype(BF16)
    across_mid = send(hidden_mid.at[c], hidden_mid.at[c], hidden_mid.at[sib], sibling)
    across.sent()
    pending.remove(across)
    pump(1, 4)
    other_down = to_other(DN0, 1536, 1024)
    arrive([across_mid])

    def all_mid():
        return hidden_mid[...].reshape(512, 1024)

    def feed_forward(t, carry):
        gate = dot(all_mid(), weight(GU0 + t * 256, 256))
        up = dot(all_mid(), weight(GU0 + 1536 + t * 256, 256))
        gate_up[:, lanes(t * 256, 256)] = gate.astype(BF16)
        gate_up[:, lanes(1536 + t * 256, 256)] = up.astype(BF16)
        result = (gate * jax.nn.sigmoid(gate) * up).astype(BF16)
        for h in range(2):
            block = 2 * t + h
            active[block % 3, :, lanes((block // 3) * 128, 128)] = result[:, h * 128 : (h + 1) * 128]
        return carry

    lax.fori_loop(0, 6, feed_forward, 0)

    plans = (
        ((grads, G_DN, 512), (grads, G_DN + 512, 512), (grads, G_DN + 1024, 512)),
        ((weights, GU0, 1024), (weights, GU0 + 1024, 1024), (weights, GU0 + 2048, 1024)),
        ((weights, QKV0, 1024), (weights, QKV0 + 1024, 1024), (grads, G_OUT, 1152)),
    )
    landing, at = {}, 0
    for unit in range(3):
        for index in range(3):
            landing[unit, index] = at
            at += plans[unit][index][2]

    def piece_column(ref, offset):
        if ref is grads:
            return offset
        return S_GU + offset - GU0 if offset >= GU0 else S_QKV + offset - QKV0

    def remaining(rotation):
        return [axis for axis in "xyz" if axis != rotation[0]]

    def add_blocks(blocks, target, size, shape):
        count = math.prod(shape)

        def body(k, carry):
            where = []
            left = k
            for extent in reversed(shape):
                where.insert(0, left % extent)
                left = left // extent
            total = blocks[0](where)
            for block in blocks[1:]:
                total = total + block(where)
            target(where, total.astype(BF16))
            return carry

        if count == 1:
            body(0, 0)
        else:
            lax.fori_loop(0, count, body, 0)

    def reader(ref, offset, size, locate):
        return lambda where: ref[locate(where) + (slice(None), lanes(offset, size))].astype(F32)

    def writer(ref, offset, size, locate):
        def store(where, value):
            ref[locate(where) + (slice(None), lanes(offset, size))] = value

        return store

    sums = {}

    def reduce_one(unit, index):
        ref, offset, size = plans[unit][index]
        rotation = ROTATIONS[index]
        first, other = rotation[0], remaining(rotation)[0]
        at = landing[unit, index]
        sums[unit, index, 1] = [
            send(
                view(ref, {first: (me[first] + 2) % 4, other: pl.ds(2 * half, 2)}, offset, size),
                got_far.at[half, :, :, :, lanes(at, size)],
                got_far.at[half, :, :, :, lanes(at, size)],
                device(moved(me, first, by)),
            )
            for by, half in ((1, 0), (3, 1))
        ]

    def reduce_two(unit, index):
        ref, offset, size = plans[unit][index]
        rotation = ROTATIONS[index]
        first, (other, last) = rotation[0], remaining(rotation)
        at = landing[unit, index]
        arrive(sums[unit, index, 1])
        out = []
        for by, half in ((1, 0), (3, 1)):
            block = (me[first] + by) % 4

            def locate(where, block=block, half=half):
                spot = {first: block, other: where[0] + 2 * half, last: where[1]}
                return tuple(spot[axis] for axis in "xyz")

            add_blocks(
                [
                    reader(ref, offset, size, locate),
                    reader(got_far, at, size, lambda where, half=half: (half, where[0], where[1])),
                ],
                writer(ref, offset, size, locate),
                size,
                (2, 4),
            )
            out.append(
                send(
                    view(ref, {first: block}, offset, size),
                    got_near.at[half, :, :, :, lanes(at, size)],
                    got_near.at[half, :, :, :, lanes(at, size)],
                    device(moved(me, first, by)),
                )
            )
        sums[unit, index, 2] = out

    def reduce_three(unit, index):
        ref, offset, size = plans[unit][index]
        rotation = ROTATIONS[index]
        first, second, third = rotation
        other, last = remaining(rotation)
        at = landing[unit, index]
        arrive(sums[unit, index, 2])

        def locate(where):
            spot = {first: me[first], other: where[0], last: where[1]}
            return tuple(spot[axis] for axis in "xyz")

        add_blocks(
            [reader(ref, offset, size, locate)]
            + [
                reader(got_near, at, size, lambda where, half=half: (half, where[0], where[1]))
                for half in range(2)
            ],
            writer(ref, offset, size, locate),
            size,
            (4, 4),
        )
        sums[unit, index, 3] = [
            send(
                view(ref, {first: me[first], second: (me[second] + by) % 4}, offset, size),
                got_two.at[by - 1, :, :, lanes(at, size)],
                got_two.at[by - 1, :, :, lanes(at, size)],
                device(moved(me, second, by)),
            )
            for by in (1, 2, 3)
        ]

    def reduce_four(unit, index):
        ref, offset, size = plans[unit][index]
        first, second, third = ROTATIONS[index]
        at = landing[unit, index]
        arrive(sums[unit, index, 3])

        def locate(where):
            spot = {first: me[first], second: me[second], third: where[0]}
            return tuple(spot[axis] for axis in "xyz")

        add_blocks(
            [reader(ref, offset, size, locate)]
            + [reader(got_two, at, size, lambda where, by=by: (by, where[0])) for by in range(3)],
            writer(ref, offset, size, locate),
            size,
            (4,),
        )
        sums[unit, index, 4] = [
            send(
                view(ref, {first: me[first], second: me[second], third: (me[third] + by) % 4}, offset, size),
                got_three.at[by - 1, :, lanes(at, size)],
                got_three.at[by - 1, :, lanes(at, size)],
                device(moved(me, third, by)),
            )
            for by in (1, 2, 3)
        ]

    y_low = y % 2
    z_first = (2, 0, 2)
    local_count = [len(inward)]
    local_pending = []

    def reduce_five(unit, index):
        ref, offset, size = plans[unit][index]
        at = landing[unit, index]
        arrive(sums[unit, index, 4])
        here = (x, y, z)
        add_blocks(
            [reader(ref, offset, size, lambda where: here)]
            + [reader(got_three, at, size, lambda where, by=by: (by,)) for by in range(3)],
            writer(ref, offset, size, lambda where: here),
            size,
            (1,),
        )
        source = ref.at[x, y, z, :, lanes(offset, size)]
        column = lanes(piece_column(ref, offset), size)
        copy = pltpu.make_async_copy(
            source, summed.at[c, y_low, z, :, column], local_sem.at[local_count[0]]
        )
        local_count[0] += 1
        copy.start()
        local_pending.append(copy)
        there = summed.at[c, y_low, z, :, column]
        beside = device({**me, "y": y + 1 - 2 * y_low})
        if index == z_first[unit]:
            sums[unit, index, 5] = [
                send(source, there, summed.at[c, y_low, (z - by + 4) % 4, :, column], device(moved(me, "z", by)))
                for by in (1, 2, 3)
            ]
        else:
            sums[unit, index, 5] = [send(source, there, summed.at[c, 1 - y_low, z, :, column], beside)]

    def reduce_six(unit, index):
        ref, offset, size = plans[unit][index]
        arrive(sums[unit, index, 5])
        column = lanes(piece_column(ref, offset), size)
        beside = device({**me, "y": y + 1 - 2 * y_low})
        if index == z_first[unit]:
            source = summed.at[c, y_low, :, :, column]
            sums[unit, index, 6] = [send(source, source, summed.at[c, 1 - y_low, :, :, column], beside)]
        else:
            source = summed.at[c, :, z, :, column]
            sums[unit, index, 6] = [
                send(source, source, summed.at[c, :, (z - by + 4) % 4, :, column], device(moved(me, "z", by)))
                for by in (1, 2, 3)
            ]

    def reduce_seven(unit, index):
        ref, offset, size = plans[unit][index]
        arrive(sums[unit, index, 6])
        column = lanes(piece_column(ref, offset), size)
        source = summed.at[c, :, :, :, column]
        sums[unit, index, 7] = [send(source, source, summed.at[sib, :, :, :, column], sibling)]

    stages = (reduce_one, reduce_two, reduce_three, reduce_four, reduce_five, reduce_six, reduce_seven)

    def reduce(unit, stage):
        if stage == 4:
            while local_pending:
                local_pending.pop().wait()
        if stage == 5:
            while local_pending:
                local_pending.pop().wait()
        for index in range(3):
            stages[stage](unit, index)

    arrive([other_down])
    flush()

    def all_cots():
        return cots[...].reshape(512, 1024)

    def cot_half(half):
        return cots[:, :, lanes(half * 512, 512, 512)].reshape(512, 512)

    def grads_own(offset, size, values):
        grads[pl.ds(2 * c, 2), :, :, :, lanes(offset, size)] = values.astype(BF16).reshape(2, 4, 4, 16, size)

    def grads_other(offset, size, values):
        weights[pl.ds(2 * sib, 2), :, :, :, lanes(offset, size)] = values.astype(BF16).reshape(2, 4, 4, 16, size)

    for t in range(2):
        values = dot_tn(active[2 * c], cots[:, :, t * 512 : (t + 1) * 512].reshape(512, 512))
        grads_own(G_DN + t * 512, 512, values)
    for t in range(2):
        values = dot_tn(active[2 * sib], cots[:, :, t * 512 : (t + 1) * 512].reshape(512, 512))
        grads_other(DN0 + t * 512, 512, values)
    grads_own(G_DN + 1024, 512, dot_tn(active[1], cot_half(c)))
    grads_other(DN0 + 1024, 512, dot_tn(active[1], cot_half(sib)))
    down_grads = send(
        view(weights, {"x": pl.ds(2 * sib, 2)}, DN0, 1536),
        view(grads, {"x": pl.ds(2 * c, 2)}, G_DN, 1536),
        view(grads, {"x": pl.ds(2 * sib, 2)}, G_DN, 1536),
        sibling,
    )

    def back_active(kind, q):
        if kind == 0:
            group = 2 * c
            values = dot_nt(all_cots(), weight_rows(2 * c + q, DN0, 1024))
        elif kind == 1:
            group = 2 * sib
            values = dot_nt(all_cots(), other_weights[q, :, :, :, 1024:2048].reshape(256, 1024))
        else:
            group = 1
            values = dot_nt(cot_half(c), weight_rows(2 * c + q, DN0 + 1024, 512)) + dot_nt(
                cot_half(sib), other_weights[q, :, :, :, 2048:2560].reshape(256, 512)
            )
        for h in range(2):
            block = 3 * (2 * q + h) + group
            pulled = values[:, h * 128 : (h + 1) * 128]
            gate = gate_up[:, lanes(block * 128, 128)].astype(F32)
            up = gate_up[:, lanes(1536 + block * 128, 128)].astype(F32)
            sigma = jax.nn.sigmoid(gate)
            back_gate = pulled * up * sigma * (1.0 + gate * (1.0 - sigma))
            gate_up[:, lanes(block * 128, 128)] = back_gate.astype(BF16)
            gate_up[:, lanes(1536 + block * 128, 128)] = (pulled * gate * sigma).astype(BF16)

    def down_back(q, carry):
        for kind in range(3):
            back_active(kind, q)
        return carry

    lax.fori_loop(0, 2, down_back, 0)
    arrive([down_grads])
    reduce(0, 0)

    def back_mid(row, carry):
        values = dot_nt(gate_up[...], weight_rows(row, GU0, 3072))
        two_parts(values, lanes(row * 256, 256))
        return carry

    lax.fori_loop(0, 4, back_mid, 0)
    across = send(part.at[sib], got_part, got_part, sibling)
    turned_lhs[...] = all_mid().T

    def gate_up_grads(t, carry):
        values = dot(turned_lhs[...], gate_up[:, lanes(t * 256, 256)])
        weights[:, :, :, :, lanes(GU0 + t * 256, 256)] = values.astype(BF16).reshape(4, 4, 4, 16, 256)
        return carry

    lax.fori_loop(0, 12, gate_up_grads, 0)
    reduce(1, 0)
    reduce(0, 1)
    arrive([across])
    back = part[c] + got_part[...]
    unit_mid, scale_mid = unit_of(middle[...])
    gains_acc[1:2, :] = jnp.sum(back * unit_mid, axis=0, keepdims=True)
    back_middle = cots[c].astype(F32) + norm_back(back, gain_mid, unit_mid, scale_mid)
    branch[c] = back_middle.astype(BF16)
    across.sent()
    pending.remove(across)
    across_branch = send(branch.at[c], branch.at[c], branch.at[sib], sibling)

    down_rows = lambda t: (
        dot(active[2 * c], weight_own(DN0 + t * 256, 256))
        + dot(active[2 * sib], weight_other(1024 + t * 256, 256))
    )
    for t in range(4):
        values = down_rows(t)
        two_parts(values, pl.ds(t * 256, 256))
    for half, load in ((c, lambda: weight_own(DN0 + 1024, 512)), (sib, lambda: weight_other(2048, 512))):
        values = dot(active[1], load())
        columns = lanes(half * 512, 512, 512)
        part[0, :, columns] += values[:256]
        part[1, :, columns] += values[256:]
    across_down = send(part.at[sib], got_down, got_down, sibling)
    across_down.arrived()
    out_low[...] = (middle[...] + part[c] + got_down[...]).astype(BF16)
    across_down.sent()
    pending.remove(across_down)
    copy_out = pltpu.make_async_copy(out_low, activations, local_sem.at[0])
    copy_out.start()
    middle[...] = back_middle
    arrive([across_branch])
    reduce(1, 1)
    reduce(0, 2)

    def all_branch():
        return branch[...].reshape(512, 1024)

    for t in range(2):
        columns = slice(t * 512, (t + 1) * 512)
        grads_own(G_OUT + t * 512, 512, dot_tn(mixed[c], branch[:, :, columns].reshape(512, 512)))
    for t in range(2):
        columns = slice(t * 512, (t + 1) * 512)
        grads_other(OUT0 + t * 512, 512, dot_tn(mixed[sib], branch[:, :, columns].reshape(512, 512)))
    out_grads = send(
        view(weights, {"x": pl.ds(2 * sib, 2)}, OUT0, 1024),
        view(grads, {"x": pl.ds(2 * c, 2)}, G_OUT, 1024),
        view(grads, {"x": pl.ds(2 * sib, 2)}, G_OUT, 1024),
        sibling,
    )
    mixed[c] = dot_nt(all_branch(), weight_own(OUT0, 1024)).astype(BF16)
    mixed[sib] = dot_nt(all_branch(), weight_other(0, 1024)).astype(BF16)
    gains_acc[2:3, :] = jnp.zeros((1, 1024), F32)

    def attend_back(step, carry):
        b, g = step // 4, step % 4
        rows, query, key, value, probs = probabilities(b, g)
        pulled = jnp.concatenate([mixed[h, rows, lanes(g * 128, 128)] for h in range(2)], axis=0)
        back_probs = dot_nt(pulled, value)
        inner = jnp.sum(probs * back_probs, axis=-1, keepdims=True)
        back_scores = (probs * (back_probs - inner) * SCALE).astype(BF16)
        back_query = dot(back_scores, key)
        back_key = dot_tn(back_scores, query)
        back_value = dot_tn(probs.astype(BF16), pulled)
        cosine = rope[b, :, 0:128]
        sine = rope[b, :, 128:256]

        def through(upstream, column, gain):
            unit, scale = unit_of(raw[rows, lanes(column, 128)].astype(F32))
            plain = upstream * cosine - pltpu.roll(upstream, 64, 1) * sine
            gate_up[rows, lanes(column, 128)] = norm_back(plain, gain, unit, scale).astype(BF16)
            return jnp.sum(plain * unit, axis=0, keepdims=True)

        for h in range(2):
            gains_acc[2:3, 0:128] += through(
                back_query[h * 256 : (h + 1) * 256], (2 * g + h) * 128, gain_query
            )
        gains_acc[2:3, 128:256] += through(back_key, 1024 + g * 128, gain_key)
        gate_up[rows, lanes(1536 + g * 128, 128)] = back_value.astype(BF16)
        return carry

    lax.fori_loop(0, 8, attend_back, 0)
    reduce(1, 2)
    reduce(0, 3)

    def back_in(row, carry):
        values = dot_nt(gate_up[:, 0:2048], weight_rows(row, QKV0, 2048))
        two_parts(values, lanes(row * 256, 256))
        return carry

    lax.fori_loop(0, 4, back_in, 0)
    across = send(part.at[sib], got_part, got_part, sibling)
    turned_lhs[...] = all_hidden().T

    def qkv_grads(t, carry):
        values = dot(turned_lhs[...], gate_up[:, lanes(t * 256, 256)])
        weights[:, :, :, :, lanes(QKV0 + t * 256, 256)] = values.astype(BF16).reshape(4, 4, 4, 16, 256)
        return carry

    lax.fori_loop(0, 8, qkv_grads, 0)
    arrive([across])
    back = part[c] + got_part[...]
    unit_in, scale_in = unit_of(toks[c].astype(F32))
    gains_acc[0:1, :] = jnp.sum(back * unit_in, axis=0, keepdims=True)
    pltpu.make_async_copy(out_low, activations, local_sem.at[0]).wait()
    out_low[...] = (middle[...] + norm_back(back, gain_in, unit_in, scale_in)).astype(BF16)
    copy_out = pltpu.make_async_copy(out_low, input_grad, local_sem.at[1])
    copy_out.start()

    low = jnp.concatenate(
        [gains_acc[r : r + 1, i * 128 : (i + 1) * 128] for r in range(2) for i in range(8)], axis=0
    ).astype(BF16)
    high = jnp.concatenate(
        [gains_acc[2:3, 0:128], gains_acc[2:3, 128:256], jnp.zeros((14, 128), F32)], axis=0
    ).astype(BF16)
    grads[:, :, :, :, G_GAIN : G_GAIN + 128] = jnp.zeros((4, 4, 4, 16, 128), BF16)
    for part_x in range(4):
        for part_y in (0, 2):
            grads[part_x, part_y, 0, :, G_GAIN : G_GAIN + 128] = low
            grads[part_x, part_y, 1, :, G_GAIN : G_GAIN + 128] = high
    arrive([out_grads])
    reduce(2, 0)
    reduce(0, 4)
    reduce(1, 3)
    reduce(0, 5)
    reduce(2, 1)
    reduce(1, 4)
    reduce(0, 6)
    reduce(2, 2)
    reduce(1, 5)
    reduce(2, 3)
    reduce(1, 6)
    reduce(2, 4)
    reduce(2, 5)
    reduce(2, 6)
    for unit in range(3):
        for index in range(3):
            arrive(sums[unit, index, 7])
    copy_out.wait()
    flush()


TRANSFERS = 256


def run_layer(tokens, cotangent, tables, bias, piece):
    anywhere = pl.BlockSpec(memory_space=pl.ANY)
    vmem = pltpu.VMEM
    return pl.pallas_call(
        layer_kernel,
        out_shape=(
            jax.ShapeDtypeStruct((TOK, D), BF16),
            jax.ShapeDtypeStruct((TOK, D), BF16),
            jax.ShapeDtypeStruct((2, 2, 4, 16, WCOLS), BF16),
        ),
        in_specs=[anywhere] * 5,
        out_specs=(anywhere,) * 3,
        scratch_shapes=[
            vmem((4, 4, 4, 16, WCOLS), BF16),
            vmem((4, 4, 4, 16, G_COLS), BF16),
            vmem((2, 4, 4, 16, 2560), BF16),
            vmem((2, 2, 4, 16, WCOLS), BF16),
            vmem((2, 4, 4, 16, WCOLS), BF16),
            vmem((3, 4, 16, WCOLS), BF16),
            vmem((3, 16, WCOLS), BF16),
            vmem((2, TOK, D), BF16),
            vmem((2, TOK, D), BF16),
            vmem((2, TOK, 256), F32),
            vmem((2, TOK, TOK), F32),
            vmem((2, TOK, D), BF16),
            vmem((2 * TOK, 1536), BF16),
            vmem((12, 2 * TOK, HD), BF16),
            vmem((4, 2 * TOK, HD), BF16),
            vmem((2, 2 * TOK, 512), BF16),
            vmem((2, TOK, D), F32),
            vmem((TOK, D), F32),
            vmem((TOK, D), F32),
            vmem((TOK, D), F32),
            vmem((2, TOK, D), BF16),
            vmem((2 * TOK, 3072), BF16),
            vmem((3, 2 * TOK, 512), BF16),
            vmem((2, TOK, D), BF16),
            vmem((D, 2 * TOK), BF16),
            vmem((TOK, D), BF16),
            vmem((8, D), F32),
            pltpu.SemaphoreType.DMA((24,)),
            pltpu.SemaphoreType.DMA((TRANSFERS,)),
            pltpu.SemaphoreType.DMA((TRANSFERS,)),
        ],
        compiler_params=pltpu.CompilerParams(
            collective_id=0, has_side_effects=True, vmem_limit_bytes=64 * 2**20
        ),
        cost_estimate=pl.CostEstimate(flops=26 * 10**9, bytes_accessed=10**7, transcendentals=10**6),
    )(tokens, cotangent, tables, bias, piece)


def adamw(master, first, second, gradient, rate, decay):
    first_new = 0.9 * first + 0.1 * gradient
    second_new = 0.999 * second + 0.001 * gradient * gradient
    direction = first_new / (1.0 - 0.9**STEP) / (jnp.sqrt(second_new / (1.0 - 0.999**STEP)) + 1e-08)
    return (master - rate * (direction + decay * master), first_new, second_new)


def per_device(
    tokens,
    cotangent,
    segment_ids,
    positions,
    master_qkv,
    master_out,
    master_gate_up,
    master_down,
    master_gains,
    first_qkv,
    first_out,
    first_gate_up,
    first_down,
    first_gains,
    second_qkv,
    second_out,
    second_gate_up,
    second_down,
    second_gains,
):
    me = coordinates()
    c = me["c"]
    shard = lax.axis_index("shard")
    order = (me["y"] % 2) * 4 + me["z"]
    row = 16 * order

    def half(array, offset, size):
        return lax.dynamic_slice(array, (row, offset + c * size), (16, size))

    down = lax.dynamic_slice(master_down.reshape(3, 128, D), (0, row, 0), (3, 16, D))
    whole = jnp.where(c == 0, down[0], down[2])
    shared = jnp.where(c == 0, down[1][:, :512], down[1][:, 512:])
    out = lax.dynamic_slice(master_out.reshape(2, 128, D), (c, row, 0), (1, 16, D))[0]
    spread = lax.dynamic_update_slice(jnp.zeros((32 * 128,), F32), master_gains, (288 * shard,))
    spread = jnp.concatenate([spread.reshape(2, 16, 128), jnp.zeros((6, 16, 128), F32)], axis=0)
    gains = lax.dynamic_slice(spread, (order, 0, 0), (1, 16, 128))[0]
    piece = jnp.concatenate(
        [
            half(master_qkv, 0, 1024),
            half(master_qkv, 2048, 512),
            half(master_qkv, 3072, 512),
            out,
            gains,
            half(master_gate_up, 0, 1536),
            half(master_gate_up, 3072, 1536),
            whole,
            shared,
        ],
        axis=1,
    ).astype(BF16)

    freq = jnp.exp(jnp.arange(HD // 2).astype(F32) * (-2.0 * math.log(1000000.0) / HD))
    angle = positions[0].astype(F32)[:, None] * freq
    cosine = jnp.cos(angle)
    sine = jnp.sin(angle)
    tables = jnp.concatenate([cosine, cosine, -sine, sine], axis=-1)
    segments = segment_ids[0]
    places = jnp.arange(TOK)
    allowed = (places[None, :] <= places[:, None]) & (segments[:, None] == segments[None, :])
    bias = jnp.where(allowed, 0.0, -1e30).astype(F32)

    activations, input_grad, summed = run_layer(tokens, cotangent, tables, bias, piece)
    summed = summed.reshape(2, 128, WCOLS)

    gradient = summed.astype(F32)
    g0, g1 = gradient[0], gradient[1]
    grad_qkv = jnp.concatenate(
        [
            g0[:, S_QKV : S_QKV + 1024],
            g1[:, S_QKV : S_QKV + 1024],
            g0[:, S_QKV + 1024 : S_QKV + 1536],
            g1[:, S_QKV + 1024 : S_QKV + 1536],
            g0[:, S_QKV + 1536 : S_QKV + 2048],
            g1[:, S_QKV + 1536 : S_QKV + 2048],
        ],
        axis=1,
    )
    grad_out = jnp.concatenate([g0[:, :1024], g1[:, :1024]], axis=0)
    grad_gate_up = jnp.concatenate(
        [
            g0[:, S_GU : S_GU + 1536],
            g1[:, S_GU : S_GU + 1536],
            g0[:, S_GU + 1536 :],
            g1[:, S_GU + 1536 :],
        ],
        axis=1,
    )
    grad_down = jnp.concatenate(
        [
            g0[:, G_DN : G_DN + 1024],
            jnp.concatenate([g0[:, G_DN + 1024 : G_DN + 1536], g1[:, G_DN + 1024 : G_DN + 1536]], axis=1),
            g1[:, G_DN : G_DN + 1024],
        ],
        axis=0,
    )
    gain_rows = (g0[:32, G_GAIN : G_GAIN + 128] + g1[:32, G_GAIN : G_GAIN + 128]).reshape(-1)
    grad_gains = lax.dynamic_slice(gain_rows, (288 * shard,), (288,))
    updated = [
        adamw(master_qkv, first_qkv, second_qkv, grad_qkv, 0.05, 0.1),
        adamw(master_out, first_out, second_out, grad_out, 0.05, 0.1),
        adamw(master_gate_up, first_gate_up, second_gate_up, grad_gate_up, 0.05, 0.1),
        adamw(master_down, first_down, second_down, grad_down, 0.05, 0.1),
        adamw(master_gains, first_gains, second_gains, grad_gains, 0.4, 0.0),
    ]
    return (
        activations,
        input_grad,
        *(new[0] for new in updated),
        *(new[1] for new in updated),
        *(new[2] for new in updated),
    )


def solution(mesh):
    rows = P(("rep", "shard"), None)
    state = (P("shard", None),) * 4 + (P("shard"),)
    return jax.shard_map(
        per_device,
        mesh=mesh,
        in_specs=(rows,) * 4 + state * 3,
        out_specs=(rows,) * 2 + state * 3,
        check_vma=False,
    )
```

time: 3300 us -> 246 us (0.07)
  waiting for transfers between devices: 2830 us -> 0 us
  blocking collectives: 217 us -> 0 us
  Pallas kernels: 0 us -> 206 us
  matrix products: 111 us -> 0 us
  local copies, waits for them, and re-layouts: 66.4 us -> 19.1 us
  other arithmetic: 54.3 us -> 18.2 us
    reduce_scatter x4 -> x0, waiting for transfers between devices: 2450 us -> none  [the longest x1 647 us: per_device(): lax.psum_scatter(regroup(grad_out, shards, replicas), ('rep', 'shard'), s...]
    all_gather x6 -> x0, waiting for transfers between devices: 378 us -> none  [the longest x1 143 us: per_device(): lax.all_gather(master_gate_up.astype(jnp.bfloat16), 'shard', axis=0, tile...]
    pallas_call x0 -> x1, Pallas kernels: none -> 206 us  [run_layer(): pl.pallas_call(layer_kernel, out_shape=(jax.ShapeDtypeStruct((TOK, D), BF...]
    unnamed x3 -> x0, blocking collectives: 152 us -> none
    dot_general x18 -> x0, matrix products: 111 us -> none  [the longest x1 11.7 us: per_device(): jnp.dot(hidden_mid.T, back_gate_up, preferred_element_type=jnp.float32)]
    all_gather x2 -> x0, blocking collectives: 65.5 us -> none  [the longest x1 33.4 us: per_device(): lax.all_gather(pieces[1].astype(jnp.bfloat16), 'rep', axis=0, tiled=True)]
    transpose x5 -> x0, local copies, waits for them, and re-layouts: 39.8 us -> none  [regroup(): return jnp.swapaxes(shaped, 0, 1).reshape(gradient.shape)]
  transfers between devices with their start and end apart: 10 -> 0, of which waited for: 10 -> 0; matrix products, arithmetic and copies ran while one was open for 4% -> 0% of each run, Pallas kernels for 0% -> 0%
where the time goes in v1:
time: 246 us; the launch traced here: 245 us
  Pallas kernels  206 us (84%)
  local copies, waits for them, and re-layouts  19.1 us (8%)
  other arithmetic  18.2 us (7%)
    pallas_call x1, Pallas kernels, run_layer(): pl.pallas_call(layer_kernel, out_shape=(jax.ShapeDtypeStruct((TOK, D), BF...  206 us
    sub x5, other arithmetic, adamw(): return (master - rate * (direction + decay * master), first_new, second_new)  14.4 us
    unnamed x47, local copies, waits for them, and re-layouts  13.8 us

profile of v1, /device:TPU:1, one launch (start us, length us, event | category | flops | bytes accessed | tf_op | source)
XLA Modules:
  0.0 244.6 jit_solution(4226533558707698096)
XLA Ops:
  0.8 0.7 convert_element_type.22
  1.5 0.9 dynamic_update_slice.3
  2.3 0.8 dynamic-slice_bitcast_fusion
  3.2 0.8 fusion.10
  4.0 0.8 constant_dynamic-update-slice_fusion.3
  4.8 0.8 constant_dynamic-update-slice_fusion.2
  5.5 0.8 fusion.12
  6.4 0.9 fusion.7
  7.3 0.9 fusion.8
  8.2 0.9 fusion.14
  9.1 0.7 copy-done.15
  9.8 0.5 multiply_cosine_fusion
  10.3 1.7 pad_maximum_fusion.3
  12.0 206.3 %shard_map.314 = (bf16[256,1024]{1,0:T(8,128)(2,1)}, bf16[256,1024]{1,0:T(8,128)(2,1)}, bf16[2,2,4,16,7808]{4,3,2,1,0:T(8,128)(2,1)}) custom-call(bf16[256,1024]{1,0:T(8,128)(2,1)} %tokens.1, bf16[256,1024]{1,0:T(8,128)(2,1)} %cotangent.1, f32[256,256]{1,0:T(8,128)} %get-tuple-element.57.tables, f32[256,256]{1,0:T(8,128)} %get-tuple-element.58.bias, ...), custom_call_target="tpu_custom_call" | custom-call | flops 25999998976 | bytes 10000000 | tf_op jit(solution)/shard_map/pallas_call | solution.py:823
  218.3 2.8 %fusion.30 = (f32[1,2,4,16,7808]{4,3,2,1,0:T(8,128)S(1)}, f32[1,2,4,16,7808]{4,3,2,1,0:T(8,128)S(1)}) fusion(bf16[2,2,4,16,7808]{4,3,2,1,0:T(8,128)(2,1)} %get-tuple-element.22), kind=kLoop, calls=%fused_computation.69 | loop fusion | bytes 15990784 | tf_op jit(solution)/shard_map/slice | solution.py:944
  221.2 0.7 multiply_subtract_fusion.4
  222.1 0.2 fusion.29
  222.8 1.0 copy-done.9
  223.8 0.3 copy-done.10
  224.1 0.3 copy-done.11
  224.5 2.3 multiply_subtract_fusion.3
  226.7 0.8 copy-done.7
  227.5 0.5 copy-done.8
  228.0 3.1 %multiply_subtract_fusion.2 = (f32[384,1024]{1,0:T(8,128)}, f32[384,1024]{1,0:T(8,128)}, f32[384,1024]{1,0:T(8,128)}) fusion(f32[384,1024]{1,0:T(8,128)S(1)} %copy-done.6, f32[128,1024]{1,0:T(8,128)S(1)} %get-tuple-element.45, f32[128,512]{1,0:T(8,128)S(1)} %get-tuple-element.43, f32[128,512]{1,0:T(8,128)S(1)} %get-tuple-element.41, ...), kind=kLoop, calls=%fused_computation.12 | loop fusion | flops 7077888 | bytes 11010048 | tf_op jit(solution)/shard_map/sub | solution.py:875
  231.0 0.7 copy-done.4
  231.7 0.8 copy-done.5
  232.5 4.0 %multiply_subtract_fusion.1 = (f32[128,4096]{1,0:T(8,128)}, f32[128,4096]{1,0:T(8,128)}, f32[128,4096]{1,0:T(8,128)}) fusion(f32[128,4096]{1,0:T(8,128)S(1)} %copy-done.3, f32[128,4096]{1,0:T(8,128)S(1)} %get-tuple-element.44, f32[128,4096]{1,0:T(8,128)S(1)} %copy-done.4, f32[128,4096]{1,0:T(8,128)S(1)} %copy-done.5), kind=kLoop, calls=%fused_computation.8 | loop fusion | flops 7864320 | bytes 14680064 | tf_op jit(solution)/shard_map/sub | solution.py:875
  236.5 1.1 copy-done.1
  237.6 0.9 copy-done.2
  238.5 4.4 %multiply_subtract_fusion = (f32[128,6144]{1,0:T(8,128)}, f32[128,6144]{1,0:T(8,128)}, f32[128,6144]{1,0:T(8,128)}) fusion(f32[128,6144]{1,0:T(8,128)S(1)} %copy-done, f32[128,1536]{1,0:T(8,128)S(1)} %get-tuple-element.51, f32[128,1536]{1,0:T(8,128)S(1)} %get-tuple-element.49, f32[128,1536]{1,0:T(8,128)S(1)} %get-tuple-element.50, ...), kind=kLoop, calls=%fused_computation.3 | loop fusion | flops 14155776 | bytes 22020096 | tf_op jit(solution)/shard_map/sub | solution.py:875
  243.0 0.8 copy.53
  243.8 0.8 copy.54
  (38 shorter events, 0.7 us)
Async XLA Ops:
  9.1 0.7 copy-start.15
  218.3 2.9 %copy-start.14 = (f32[288]{0:T(512)S(1)}, f32[288]{0:T(512)}, u32[]{:S(2)}) copy-start(f32[288]{0:T(512)} %param.27) | copy-start | bytes 3460
  218.3 2.9 %copy-start.16 = (f32[288]{0:T(512)S(1)}, f32[288]{0:T(512)}, u32[]{:S(2)}) copy-start(f32[288]{0:T(512)} %param.32) | copy-start | bytes 3460
  218.3 2.9 %copy-start.17 = (f32[288]{0:T(512)S(1)}, f32[288]{0:T(512)}, u32[]{:S(2)}) copy-start(f32[288]{0:T(512)} %param.37) | copy-start | bytes 3460
  222.6 1.2 copy-start.9
  222.6 1.5 copy-start.10
  222.6 1.8 copy-start.11
  224.5 2.3 copy-start.6
  224.5 3.0 %copy-start.7 = (f32[384,1024]{1,0:T(8,128)S(1)}, f32[384,1024]{1,0:T(8,128)}, u32[]{:S(2)}) copy-start(f32[384,1024]{1,0:T(8,128)} %param.31) | copy-start | bytes 4718596
  224.5 3.5 %copy-start.8 = (f32[384,1024]{1,0:T(8,128)S(1)}, f32[384,1024]{1,0:T(8,128)}, u32[]{:S(2)}) copy-start(f32[384,1024]{1,0:T(8,128)} %param.36) | copy-start | bytes 4718596
  228.0 3.1 %copy-start.3 = (f32[128,4096]{1,0:T(8,128)S(1)}, f32[128,4096]{1,0:T(8,128)}, u32[]{:S(2)}) copy-start(f32[128,4096]{1,0:T(8,128)} %param.23) | copy-start | bytes 6291460
  228.0 3.8 %copy-start.4 = (f32[128,4096]{1,0:T(8,128)S(1)}, f32[128,4096]{1,0:T(8,128)}, u32[]{:S(2)}) copy-start(f32[128,4096]{1,0:T(8,128)} %param.28) | copy-start | bytes 6291460
  228.0 4.6 %copy-start.5 = (f32[128,4096]{1,0:T(8,128)S(1)}, f32[128,4096]{1,0:T(8,128)}, u32[]{:S(2)}) copy-start(f32[128,4096]{1,0:T(8,128)} %param.33) | copy-start | bytes 6291460
  232.5 4.0 %copy-start = (f32[128,6144]{1,0:T(8,128)S(1)}, f32[128,6144]{1,0:T(8,128)}, u32[]{:S(2)}) copy-start(f32[128,6144]{1,0:T(8,128)} %param.25) | copy-start | bytes 9437188
  232.5 5.1 %copy-start.1 = (f32[128,6144]{1,0:T(8,128)S(1)}, f32[128,6144]{1,0:T(8,128)}, u32[]{:S(2)}) copy-start(f32[128,6144]{1,0:T(8,128)} %param.30) | copy-start | bytes 9437188
  232.5 6.0 %copy-start.2 = (f32[128,6144]{1,0:T(8,128)S(1)}, f32[128,6144]{1,0:T(8,128)}, u32[]{:S(2)}) copy-start(f32[128,6144]{1,0:T(8,128)} %param.35) | copy-start | bytes 9437188
  238.5 4.4 %copy-start.13 = (bf16[256,1024]{1,0:T(8,128)(2,1)S(1)}, bf16[256,1024]{1,0:T(8,128)(2,1)}, u32[]{:S(2)}) copy-start(bf16[256,1024]{1,0:T(8,128)(2,1)} %get-tuple-element.76) | copy-start | bytes 1572868
  238.5 5.2 %copy-start.12 = (bf16[256,1024]{1,0:T(8,128)(2,1)S(1)}, bf16[256,1024]{1,0:T(8,128)(2,1)}, u32[]{:S(2)}) copy-start(bf16[256,1024]{1,0:T(8,128)(2,1)} %get-tuple-element.77) | copy-start | bytes 1572868

commit v2 on v1

v2 whole, which is shorter than its diff:
```python
import math

import jax
import jax.numpy as jnp
from jax import lax
from jax.experimental import pallas as pl
from jax.experimental.pallas import tpu as pltpu
from jax.sharding import PartitionSpec as P

D = 1024
HEADS = 16
KV_HEADS = 8
HD = 128
FF = 3072
STEP = 10
Q_WIDTH = 2048
KV_WIDTH = 1024
TOK = 256
F32 = jnp.float32
BF16 = jnp.bfloat16
EPS = 1e-06
SCALE = HD ** (-0.5)

QKV0, GAIN0, OUT0, GU0, DN0, WCOLS = 0, 2048, 2176, 3200, 6272, 7808
G_OUT, G_DN, G_COLS = 0, 1024, 2560
S_GU, S_QKV, S_GAIN, S_DN, S_OUT, S_COLS = 0, 3072, 5120, 5632, 7168, 8192
LOG2E = 1.4426950408889634
ROTATIONS = (("x", "y", "z"), ("y", "z", "x"), ("z", "x", "y"))

SCHEDULE = {
    "start": ("W0", "W1", "W2"),
    "early": ("W0", "W0", "W1", "W0", "W1", "W2"),
    "attend": ("W1",),
    "mid": ("W2",),
    "feed1": ("W2",),
    "active0": ("G0",),
    "mid1": ("G0",),
    "gu1": ("G1",),
    "output": ("G0",),
    "mixed": ("G2",),
    "attend0": ("G1", "G3", "G0"),
    "query": ("G2",),
    "key": ("G1",),
    "in": ("G3", "G4", "G0"),
    "end": tuple("G" + unit for unit in "25136402561342536142536456"),
}


def dot(left, right):
    return jnp.dot(left, right, preferred_element_type=F32)


def dot_nt(left, right):
    return lax.dot_general(left, right, (((1,), (1,)), ((), ())), preferred_element_type=F32)


def dot_tn(left, right):
    return lax.dot_general(left, right, (((0,), (0,)), ((), ())), preferred_element_type=F32)


def lanes(start, size, step=128):
    return pl.ds(start if isinstance(start, int) else pl.multiple_of(start, step), size)


def coordinates():
    rep = lax.axis_index("rep")
    shard = lax.axis_index("shard")
    return {
        "x": shard // 2,
        "y": (shard % 2) * 2 + (rep // 2) % 2,
        "z": rep // 4,
        "c": rep % 2,
    }


def device(at):
    return {"rep": at["z"] * 4 + (at["y"] % 2) * 2 + at["c"], "shard": at["x"] * 2 + at["y"] // 2}


def moved(me, axis, by):
    return {**me, axis: (me[axis] + by + 4) % 4}


def view(ref, select, offset, size):
    where = tuple(select.get(axis, slice(None)) for axis in "xyz")
    return ref.at[where + (slice(None), lanes(offset, size))]


def layer_kernel(
    tokens,
    cotangent,
    tables,
    segments,
    gains,
    master_qkv,
    master_out,
    master_gate_up,
    master_down,
    activations,
    input_grad,
    summed,
    weights,
    grads,
    other_weights,
    got_far,
    got_near,
    got_two,
    got_three,
    toks,
    cots,
    rope,
    mask,
    mask_turned,
    hidden,
    raw,
    rotated,
    vals,
    mixed,
    part,
    got_part,
    got_down,
    middle,
    hidden_mid,
    gate_up,
    active,
    branch,
    turned_lhs,
    spare,
    gains_acc,
    local_sem,
    send_sem,
    recv_sem,
):
    me = coordinates()
    c = me["c"]
    sib = 1 - c
    x, y, z = me["x"], me["y"], me["z"]
    sibling = device({**me, "c": sib})
    used = [0]

    class Transfer:
        def __init__(self, source, there, here, target):
            self.index = used[0]
            used[0] += 1
            self.source, self.there, self.here, self.target = source, there, here, target
            self.copy(source, there).start()

        def copy(self, source, there):
            return pltpu.make_async_remote_copy(
                src_ref=source,
                dst_ref=there,
                send_sem=send_sem.at[self.index],
                recv_sem=recv_sem.at[self.index],
                device_id=self.target,
                device_id_type=pl.DeviceIdType.MESH,
            )

        def arrived(self):
            self.copy(self.here, self.here).wait_recv()

        def sent(self):
            self.copy(self.source, self.there).wait_send()

    pending = []

    def send(source, there, here, target):
        transfer = Transfer(source, there, here, target)
        pending.append(transfer)
        return transfer

    def flush():
        while pending:
            pending.pop(0).sent()

    def arrive(transfers):
        for transfer in transfers:
            transfer.arrived()

    row = 16 * ((y % 2) * 4 + z)

    def rows_of(ref, first, offset, size):
        return ref.at[pl.ds(pl.multiple_of(first, 16), 16), lanes(offset, size)]

    groups = [
        (rows_of(master_qkv, row, c * 1024, 1024), QKV0, 1024),
        (rows_of(master_qkv, row, 2048 + c * 512, 512), QKV0 + 1024, 512),
        (rows_of(master_qkv, row, 3072 + c * 512, 512), QKV0 + 1536, 512),
        (rows_of(master_out, c * 128 + row, 0, 1024), OUT0, 1024),
        (rows_of(master_gate_up, row, c * 1536, 768), GU0, 768),
        (rows_of(master_gate_up, row, 3072 + c * 1536, 768), GU0 + 768, 768),
        (rows_of(master_gate_up, row, c * 1536 + 768, 768), GU0 + 1536, 768),
        (rows_of(master_gate_up, row, 3072 + c * 1536 + 768, 768), GU0 + 2304, 768),
        (rows_of(master_down, c * 256 + row, 0, 1024), DN0, 1024),
        (rows_of(master_down, 128 + row, c * 512, 512), DN0 + 1024, 512),
    ]
    inward = [
        (source, got_part.at[pl.ds(16 * index, 16), pl.ds(0, size)])
        for index, (source, offset, size) in enumerate(groups)
    ]
    inward += [(gains, got_part.at[pl.ds(160, 16), pl.ds(0, 128)])]
    first_inward = len(inward)
    inward += [
        (tables, got_down.at[:, pl.ds(0, 128)]),
        (segments, got_down.at[pl.ds(0, 8), pl.ds(128, 256)]),
        (tokens, toks.at[c]),
        (cotangent, cots.at[c]),
    ]
    inward = [pltpu.make_async_copy(*pair, local_sem.at[index]) for index, pair in enumerate(inward)]

    barrier = pltpu.get_barrier_semaphore()
    across_y = {**me, "y": y + 1 - 2 * (y % 2)}
    friends = [sibling] + [device(moved(me, axis, by)) for axis in "xyz" for by in (1, 2, 3)]
    friends += [device(moved(across_y, "z", by)) for by in (1, 2, 3)]
    for friend in friends:
        pl.semaphore_signal(barrier, inc=1, device_id=friend, device_id_type=pl.DeviceIdType.MESH)
    for copy in inward:
        copy.start()
    for copy in inward[:first_inward]:
        copy.wait()
    for index, (source, offset, size) in enumerate(groups):
        rows16 = got_part[16 * index : 16 * index + 16, 0:size]
        weights[x, y, z, :, offset : offset + size] = rows16.astype(BF16)
    weights[x, y, z, :, GAIN0 : GAIN0 + 128] = got_part[160:176, 0:128].astype(BF16)
    pl.semaphore_wait(barrier, len(friends))

    def gather_one(rotation, offset, size):
        first, second, third = rotation
        source = view(weights, {"x": x, "y": y, "z": z}, offset, size)
        out = []
        for by in (1, 2, 3):
            here = view(weights, {**{"x": x, "y": y, "z": z}, third: (me[third] - by + 4) % 4}, offset, size)
            out.append(send(source, source, here, device(moved(me, third, by))))
        return out

    def gather_two(rotation, offset, size):
        first, second, third = rotation
        source = view(weights, {first: me[first], second: me[second]}, offset, size)
        out = []
        for by in (1, 2, 3):
            here = view(weights, {first: me[first], second: (me[second] - by + 4) % 4}, offset, size)
            out.append(send(source, source, here, device(moved(me, second, by))))
        return out

    def gather_three(rotation, offset, size):
        first = rotation[0]
        source = view(weights, {first: me[first]}, offset, size)
        out = []
        for by in (1, 3):
            here = view(weights, {first: (me[first] - by + 4) % 4}, offset, size)
            out.append(send(source, source, here, device(moved(me, first, by))))
        return out

    def gather_four(rotation, offset, size):
        first, second = rotation[0], rotation[1]
        out = []
        for by, half in ((1, 0), (3, 1)):
            rows = pl.ds(2 * half, 2)
            source = view(weights, {first: (me[first] - by + 4) % 4, second: rows}, offset, size)
            here = view(weights, {first: (me[first] + 2) % 4, second: rows}, offset, size)
            out.append(send(source, source, here, device(moved(me, first, by))))
        return out

    chunks = (
        ((0, 1152), (1152, 1024), (OUT0, 1024)),
        ((GU0, 1024), (GU0 + 1024, 1024), (GU0 + 2048, 1024)),
        ((DN0, 512), (DN0 + 512, 512), (DN0 + 1024, 512)),
    )
    steps = (gather_one, gather_two, gather_three, gather_four)
    flying = [[None] * 3 for _ in chunks]

    w_step = [0] * len(chunks)
    g_stage = [0] * 7

    def pump(chunk):
        step = w_step[chunk]
        w_step[chunk] += 1
        for index, rotation in enumerate(ROTATIONS):
            if step:
                arrive(flying[chunk][index])
            if step < 4:
                flying[chunk][index] = steps[step](rotation, *chunks[chunk][index])

    def gathered(chunk):
        while w_step[chunk] < 5:
            pump(chunk)

    def exchange(name):
        for item in SCHEDULE.get(name, ()):
            (pump if item[0] == "W" else reduce)(int(item[1]))

    exchange("start")
    for copy in inward[first_inward:]:
        copy.wait()
    wave = got_down[:, 0:128]
    rope[c, :, 0:128] = jnp.concatenate([wave[:, :64], wave[:, :64]], axis=1)
    rope[c, :, 128:256] = jnp.concatenate([-wave[:, 64:], wave[:, 64:]], axis=1)
    across_segments = jnp.broadcast_to(got_down[0:1, 128:384], (256, 256))
    same = across_segments == across_segments.T
    earlier = lax.broadcasted_iota(jnp.int32, (256, 256), 1) <= lax.broadcasted_iota(
        jnp.int32, (256, 256), 0
    )
    mask[c] = jnp.where(same & earlier, 0.0, -1e30).astype(BF16)
    early = [
        send(toks.at[c], toks.at[c], toks.at[sib], sibling),
        send(rope.at[c], rope.at[c], rope.at[sib], sibling),
        send(mask.at[c], mask.at[c], mask.at[sib], sibling),
        send(cots.at[c], cots.at[c], cots.at[sib], sibling),
    ]
    exchange("early")
    arrive(early)
    for b in range(2):
        mask_turned[b] = mask[b].astype(F32).T.astype(BF16)
    exchange("late")
    gathered(0)

    def to_other(offset, size, at):
        return send(
            view(weights, {"x": pl.ds(2 * sib, 2)}, offset, size),
            view(other_weights, {}, at, size),
            view(other_weights, {}, at, size),
            sibling,
        )

    other_out = to_other(OUT0, 1024, 0)

    def weight(offset, size):
        return weights[:, :, :, :, lanes(offset, size)].reshape(1024, size)

    def weight_rows(row, offset, size):
        return weights[row, :, :, :, lanes(offset, size)].reshape(256, size)

    def weight_own(offset, size):
        return weights[pl.ds(2 * c, 2), :, :, :, lanes(offset, size)].reshape(512, size)

    def weight_other(offset, size):
        return other_weights[:, :, :, :, lanes(offset, size)].reshape(512, size)

    gain_rows = jnp.zeros((16, 128), F32)
    head_rows = jnp.zeros((16, 128), F32)
    for part_x in range(4):
        for part_y in (0, 2):
            gain_rows += weights[part_x, part_y, 0, :, pl.ds(GAIN0, 128)].astype(F32)
            head_rows += weights[part_x, part_y, 1, :, pl.ds(GAIN0, 128)].astype(F32)
    gain_in = jnp.concatenate([gain_rows[i : i + 1] for i in range(8)], axis=1)
    gain_mid = jnp.concatenate([gain_rows[i : i + 1] for i in range(8, 16)], axis=1)
    gain_query = head_rows[0:1]
    gain_key = head_rows[1:2]

    def unit_of(values):
        scale = lax.rsqrt(jnp.mean(values * values, axis=-1, keepdims=True) + EPS)
        return values * scale, scale

    def norm_back(upstream, gain, unit, scale):
        pushed = upstream * gain
        inner = jnp.mean(pushed * unit, axis=-1, keepdims=True)
        return scale * (pushed - unit * inner)

    for b in range(2):
        unit, _ = unit_of(toks[b].astype(F32))
        hidden[b] = (unit * gain_in).astype(BF16)

    def all_hidden():
        return hidden[...].reshape(512, 1024)

    mean_of = jnp.full((128, 128), 1.0 / 128, BF16)

    def head_mean(values):
        return dot(values.astype(BF16), mean_of)

    def project_heads(t, carry):
        values = dot(all_hidden(), weight(QKV0 + t * 256, 256))
        raw[:, lanes(t * 256, 256)] = values.astype(BF16)
        gain = jnp.where(t < 4, gain_query, gain_key)
        cosine = rope[:, :, 0:128].reshape(512, 128)
        sine = rope[:, :, 128:256].reshape(512, 128)
        for h in range(2):
            head = values[:, h * 128 : (h + 1) * 128]
            normal = head * lax.rsqrt(head_mean(head * head) + EPS) * gain
            rotated[2 * t + h] = (normal * cosine + pltpu.roll(normal, 64, 1) * sine).astype(BF16)
        return carry

    lax.fori_loop(0, 6, project_heads, 0)

    def project_values(t, carry):
        values = dot(all_hidden(), weight(QKV0 + 1536 + t * 256, 256)).astype(BF16)
        vals[2 * t] = values[:, :128]
        vals[2 * t + 1] = values[:, 128:]
        return carry

    lax.fori_loop(0, 2, project_values, 0)
    exchange("project")

    def heads_of(b, g):
        rows = pl.ds(pl.multiple_of(b * 256, 256), 256)
        query = rotated[pl.ds(2 * g, 2), rows, :].reshape(512, 128)
        return rows, query, rotated[8 + g, rows, :], vals[g, rows, :]

    def attend(step, carry):
        b, g = step // 4, step % 4
        rows, query, key, value = heads_of(b, g)
        scores = dot_nt(query, key).reshape(2, 256, 256) * (SCALE * LOG2E) + mask[b].astype(F32)[None]
        expo = jnp.exp2(scores).reshape(512, 256).astype(BF16)
        result = dot(expo, jnp.concatenate([value, jnp.ones((256, 128), BF16)], axis=1))
        result = (result[:, :128] / result[:, 128:]).astype(BF16)
        for h in range(2):
            mixed[h, rows, lanes(g * 128, 128)] = result[h * 256 : (h + 1) * 256]
        return carry

    lax.fori_loop(0, 8, attend, 0)

    exchange("attend")
    arrive([other_out])

    def two_parts(values, columns):
        part[0, :, columns] = values[:256]
        part[1, :, columns] = values[256:]

    def project_out(t, carry):
        values = dot(mixed[c], weight_own(OUT0 + t * 256, 256)) + dot(
            mixed[sib], weight_other(t * 256, 256)
        )
        two_parts(values, lanes(t * 256, 256))
        return carry

    lax.fori_loop(0, 4, project_out, 0)
    exchange("projected")
    across = send(part.at[sib], got_part, got_part, sibling)
    across.arrived()
    middle[...] = toks[c].astype(F32) + part[c] + got_part[...]
    unit_mid, _ = unit_of(middle[...])
    hidden_mid[c] = (unit_mid * gain_mid).astype(BF16)
    across_mid = send(hidden_mid.at[c], hidden_mid.at[c], hidden_mid.at[sib], sibling)
    across.sent()
    pending.remove(across)
    exchange("mid")
    gathered(1)
    arrive([across_mid])

    def all_mid():
        return hidden_mid[...].reshape(512, 1024)

    def feed_forward(t, carry):
        column = (t // 3) * 1536 + (t % 3) * 256
        gate = dot(all_mid(), weight(GU0 + column, 256))
        up = dot(all_mid(), weight(GU0 + column + 768, 256))
        gate_up[:, lanes(column, 256)] = gate.astype(BF16)
        gate_up[:, lanes(column + 768, 256)] = up.astype(BF16)
        result = (gate * jax.nn.sigmoid(gate) * up).astype(BF16)
        for h in range(2):
            block = 2 * t + h
            active[block % 3, :, lanes((block // 3) * 128, 128)] = result[:, h * 128 : (h + 1) * 128]
        return carry

    lax.fori_loop(0, 3, feed_forward, 0)
    exchange("feed0")
    lax.fori_loop(3, 6, feed_forward, 0)
    exchange("feed1")

    def unit_of_parts(ref, offset, sizes, column):
        parts = []
        for size in sizes:
            parts.append((ref, offset, size, column))
            offset, column = offset + size, column + size
        return parts

    plans = (
        unit_of_parts(grads, G_DN, (512, 512, 512), S_DN),
        unit_of_parts(weights, GU0, (512, 512, 512), S_GU),
        unit_of_parts(weights, GU0 + 1536, (512, 512, 512), S_GU + 1536),
        unit_of_parts(grads, G_OUT, (384, 384, 256), S_OUT),
        unit_of_parts(weights, OUT0, (384, 384, 256), S_QKV),
        unit_of_parts(weights, DN0, (384, 384, 256), S_QKV + 1024),
        unit_of_parts(weights, DN0 + 1024, (128,), S_GAIN),
    )
    UNITS = len(plans)
    landing, at = {}, 0
    for unit in range(UNITS):
        for index in range(len(plans[unit])):
            landing[unit, index] = at
            at += plans[unit][index][2]

    def remaining(rotation):
        return [axis for axis in "xyz" if axis != rotation[0]]

    def add_blocks(blocks, target, size, shape):
        count = math.prod(shape)

        def body(k, carry):
            where = []
            left = k
            for extent in reversed(shape):
                where.insert(0, left % extent)
                left = left // extent
            total = blocks[0](where)
            for block in blocks[1:]:
                total = total + block(where)
            target(where, total.astype(BF16))
            return carry

        if count == 1:
            body(0, 0)
        else:
            lax.fori_loop(0, count, body, 0)

    def reader(ref, offset, size, locate):
        return lambda where: ref[locate(where) + (slice(None), lanes(offset, size))].astype(F32)

    def writer(ref, offset, size, locate):
        def store(where, value):
            ref[locate(where) + (slice(None), lanes(offset, size))] = value

        return store

    sums = {}

    def reduce_one(unit, index):
        ref, offset, size, to = plans[unit][index]
        rotation = ROTATIONS[index]
        first, other = rotation[0], remaining(rotation)[0]
        at = landing[unit, index]
        sums[unit, index, 1] = [
            send(
                view(ref, {first: (me[first] + 2) % 4, other: pl.ds(2 * half, 2)}, offset, size),
                got_far.at[half, :, :, :, lanes(at, size)],
                got_far.at[half, :, :, :, lanes(at, size)],
                device(moved(me, first, by)),
            )
            for by, half in ((1, 0), (3, 1))
        ]

    def reduce_two(unit, index):
        ref, offset, size, to = plans[unit][index]
        rotation = ROTATIONS[index]
        first, (other, last) = rotation[0], remaining(rotation)
        at = landing[unit, index]
        arrive(sums[unit, index, 1])
        out = []
        for by, half in ((1, 0), (3, 1)):
            block = (me[first] + by) % 4

            def locate(where, block=block, half=half):
                spot = {first: block, other: where[0] + 2 * half, last: where[1]}
                return tuple(spot[axis] for axis in "xyz")

            add_blocks(
                [
                    reader(ref, offset, size, locate),
                    reader(got_far, at, size, lambda where, half=half: (half, where[0], where[1])),
                ],
                writer(ref, offset, size, locate),
                size,
                (2, 4),
            )
            out.append(
                send(
                    view(ref, {first: block}, offset, size),
                    got_near.at[half, :, :, :, lanes(at, size)],
                    got_near.at[half, :, :, :, lanes(at, size)],
                    device(moved(me, first, by)),
                )
            )
        sums[unit, index, 2] = out

    def reduce_three(unit, index):
        ref, offset, size, to = plans[unit][index]
        rotation = ROTATIONS[index]
        first, second, third = rotation
        other, last = remaining(rotation)
        at = landing[unit, index]
        arrive(sums[unit, index, 2])

        def locate(where):
            spot = {first: me[first], other: where[0], last: where[1]}
            return tuple(spot[axis] for axis in "xyz")

        add_blocks(
            [reader(ref, offset, size, locate)]
            + [
                reader(got_near, at, size, lambda where, half=half: (half, where[0], where[1]))
                for half in range(2)
            ],
            writer(ref, offset, size, locate),
            size,
            (4, 4),
        )
        sums[unit, index, 3] = [
            send(
                view(ref, {first: me[first], second: (me[second] + by) % 4}, offset, size),
                got_two.at[by - 1, :, :, lanes(at, size)],
                got_two.at[by - 1, :, :, lanes(at, size)],
                device(moved(me, second, by)),
            )
            for by in (1, 2, 3)
        ]

    def reduce_four(unit, index):
        ref, offset, size, to = plans[unit][index]
        first, second, third = ROTATIONS[index]
        at = landing[unit, index]
        arrive(sums[unit, index, 3])

        def locate(where):
            spot = {first: me[first], second: me[second], third: where[0]}
            return tuple(spot[axis] for axis in "xyz")

        add_blocks(
            [reader(ref, offset, size, locate)]
            + [reader(got_two, at, size, lambda where, by=by: (by, where[0])) for by in range(3)],
            writer(ref, offset, size, locate),
            size,
            (4,),
        )
        sums[unit, index, 4] = [
            send(
                view(ref, {first: me[first], second: me[second], third: (me[third] + by) % 4}, offset, size),
                got_three.at[by - 1, :, lanes(at, size)],
                got_three.at[by - 1, :, lanes(at, size)],
                device(moved(me, third, by)),
            )
            for by in (1, 2, 3)
        ]

    y_low = y % 2
    ways = ("yz", "yz", "zy", "yz", "all", "all", "all")
    local_count = [len(inward)]
    local_pending = {}

    def whole(unit):
        ref, offset, _, to = plans[unit][0]
        size = sum(part[2] for part in plans[unit])
        return ref.at[x, y, z, :, lanes(offset, size)], lanes(to, size)

    def along_z(unit, number, source, there, here):
        sums[unit, number] = [
            send(source, there, here((z - by + 4) % 4), device(moved(me, "z", by))) for by in (1, 2, 3)
        ]

    def reduce_five(unit):
        for index in range(len(plans[unit])):
            ref, offset, size, to = plans[unit][index]
            at = landing[unit, index]
            arrive(sums[unit, index, 4])
            here = (x, y, z)
            add_blocks(
                [reader(ref, offset, size, lambda where: here)]
                + [reader(got_three, at, size, lambda where, by=by: (by,)) for by in range(3)],
                writer(ref, offset, size, lambda where: here),
                size,
                (1,),
            )
        source, column = whole(unit)
        there = summed.at[c, y_low, z, :, column]
        local_pending[unit] = pltpu.make_async_copy(source, there, local_sem.at[local_count[0]])
        local_count[0] += 1
        local_pending[unit].start()
        if ways[unit] != "yz":
            along_z(unit, 5, source, there, lambda at_z: summed.at[c, y_low, at_z, :, column])
        if ways[unit] == "yz":
            sums[unit, 5] = [send(source, there, summed.at[c, 1 - y_low, z, :, column], device(across_y))]
        if ways[unit] == "all":
            sums[unit, 5] += [
                send(
                    source,
                    there,
                    summed.at[c, 1 - y_low, (z - by + 4) % 4, :, column],
                    device(moved(across_y, "z", by)),
                )
                for by in range(4)
            ]

    def reduce_six(unit):
        if ways[unit] == "all":
            return
        source, column = whole(unit)
        arrive(sums[unit, 5])
        local_pending.pop(unit).wait()
        if ways[unit] == "zy":
            source = summed.at[c, y_low, :, :, column]
            sums[unit, 6] = [send(source, source, summed.at[c, 1 - y_low, :, :, column], device(across_y))]
        else:
            source = summed.at[c, :, z, :, column]
            along_z(unit, 6, source, source, lambda at_z: summed.at[c, :, at_z, :, column])

    def reduce_seven(unit):
        if ways[unit] == "all":
            arrive(sums[unit, 5])
            local_pending.pop(unit).wait()
        else:
            arrive(sums[unit, 6])
        source, column = whole(unit)
        source = summed.at[c, :, :, :, column]
        sums[unit, 7] = [send(source, source, summed.at[sib, :, :, :, column], sibling)]

    stages = (reduce_one, reduce_two, reduce_three, reduce_four, reduce_five, reduce_six, reduce_seven)

    def reduce(unit):
        stage = g_stage[unit]
        g_stage[unit] += 2 if stage == 4 and ways[unit] == "all" else 1
        if stage >= 4:
            stages[stage](unit)
        else:
            for index in range(len(plans[unit])):
                stages[stage](unit, index)

    def all_cots():
        return cots[...].reshape(512, 1024)

    def cot_half(half):
        return cots[:, :, lanes(half * 512, 512, 512)].reshape(512, 512)

    def grads_own(offset, size, values):
        grads[pl.ds(2 * c, 2), :, :, :, lanes(offset, size)] = values.astype(BF16).reshape(2, 4, 4, 16, size)

    def grads_other(offset, size, values):
        weights[pl.ds(2 * sib, 2), :, :, :, lanes(offset, size)] = values.astype(BF16).reshape(2, 4, 4, 16, size)

    def turned(values, t):
        turned_lhs[pl.ds(2 * t, 2)] = values.astype(BF16).reshape(2, 4, 4, 16, 512)

    for t in range(2):
        columns = slice(t * 512, (t + 1) * 512)
        turned(dot_tn(active[2 * sib], cots[:, :, columns].reshape(512, 512)), t)
    spare[...] = dot_tn(active[1], cot_half(sib)).astype(BF16).reshape(2, 4, 4, 16, 512)
    to_sibling = [
        send(source, view(grads, {"x": pl.ds(2 * c, 2)}, at, 512), view(grads, {"x": pl.ds(2 * sib, 2)}, at, 512), sibling)
        for source, at in (
            (turned_lhs.at[0:2], G_DN),
            (turned_lhs.at[2:4], G_DN + 512),
            (spare, G_DN + 1024),
        )
    ]
    for t in range(2):
        values = dot_tn(active[2 * c], cots[:, :, t * 512 : (t + 1) * 512].reshape(512, 512))
        grads_own(G_DN + t * 512, 512, values)
    grads_own(G_DN + 1024, 512, dot_tn(active[1], cot_half(c)))
    exchange("down")
    arrive(to_sibling)
    reduce(0)
    gathered(2)
    other_down = to_other(DN0, 1536, 1024)
    flush()
    turned_lhs[...] = all_mid().T.reshape(4, 4, 4, 16, 512)
    arrive([other_down])

    def left():
        return turned_lhs[...].reshape(1024, 512)

    def back_active(kind, q):
        if kind == 0:
            group = 2 * c
            values = dot_nt(all_cots(), weight_rows(2 * c + q, DN0, 1024))
        elif kind == 1:
            group = 2 * sib
            values = dot_nt(all_cots(), other_weights[q, :, :, :, 1024:2048].reshape(256, 1024))
        else:
            group = 1
            values = dot_nt(cot_half(c), weight_rows(2 * c + q, DN0 + 1024, 512)) + dot_nt(
                cot_half(sib), other_weights[q, :, :, :, 2048:2560].reshape(256, 512)
            )
        for h in range(2):
            column = q * 1536 + (3 * h + group) * 128
            pulled = values[:, h * 128 : (h + 1) * 128]
            gate = gate_up[:, lanes(column, 128)].astype(F32)
            up = gate_up[:, lanes(column + 768, 128)].astype(F32)
            sigma = jax.nn.sigmoid(gate)
            back_gate = pulled * up * sigma * (1.0 + gate * (1.0 - sigma))
            gate_up[:, lanes(column, 128)] = back_gate.astype(BF16)
            gate_up[:, lanes(column + 768, 128)] = (pulled * gate * sigma).astype(BF16)

    def back_mid(half):
        def body(row, carry):
            values = dot_nt(
                gate_up[:, half * 1536 : (half + 1) * 1536], weight_rows(row, GU0 + half * 1536, 1536)
            )
            columns = lanes(row * 256, 256)
            if half == 0:
                two_parts(values, columns)
            else:
                part[0, :, columns] += values[:256]
                part[1, :, columns] += values[256:]
            return carry

        lax.fori_loop(0, 4, body, 0)

    def gate_up_grads(half):
        def body(t, carry):
            column = half * 1536 + t * 256
            values = dot(left(), gate_up[:, lanes(column, 256)])
            weights[:, :, :, :, lanes(GU0 + column, 256)] = values.astype(BF16).reshape(4, 4, 4, 16, 256)
            return carry

        lax.fori_loop(0, 6, body, 0)

    for kind in range(3):
        back_active(kind, 0)
    exchange("active0")
    back_mid(0)
    gate_up_grads(0)
    reduce(1)
    exchange("gu0")
    for kind in range(3):
        back_active(kind, 1)
    exchange("active1")
    back_mid(1)
    exchange("mid1")
    across = send(part.at[sib], got_part, got_part, sibling)
    gate_up_grads(1)
    reduce(2)
    exchange("gu1")
    arrive([across])
    back = part[c] + got_part[...]
    unit_mid, scale_mid = unit_of(middle[...])
    gains_acc[1:2, :] = jnp.sum(back * unit_mid, axis=0, keepdims=True)
    back_middle = cots[c].astype(F32) + norm_back(back, gain_mid, unit_mid, scale_mid)
    branch[c] = back_middle.astype(BF16)
    across.sent()
    pending.remove(across)
    across_branch = send(branch.at[c], branch.at[c], branch.at[sib], sibling)
    cots[c] = (back_middle - branch[c].astype(F32)).astype(BF16)

    down_rows = lambda t: (
        dot(active[2 * c], weight_own(DN0 + t * 256, 256))
        + dot(active[2 * sib], weight_other(1024 + t * 256, 256))
    )
    for t in range(4):
        values = down_rows(t)
        two_parts(values, pl.ds(t * 256, 256))
    for half, load in ((c, lambda: weight_own(DN0 + 1024, 512)), (sib, lambda: weight_other(2048, 512))):
        values = dot(active[1], load())
        columns = lanes(half * 512, 512, 512)
        part[0, :, columns] += values[:256]
        part[1, :, columns] += values[256:]
    across_down = send(part.at[sib], got_down, got_down, sibling)
    middle[...] += part[c]
    exchange("output")
    arrive([across_branch])

    def all_branch():
        return branch[...].reshape(512, 1024)

    for t in range(2):
        columns = slice(t * 512, (t + 1) * 512)
        turned(dot_tn(mixed[sib], branch[:, :, columns].reshape(512, 512)), t)
    to_sibling = [
        send(
            turned_lhs.at[2 * t : 2 * t + 2],
            view(grads, {"x": pl.ds(2 * c, 2)}, G_OUT + t * 512, 512),
            view(grads, {"x": pl.ds(2 * sib, 2)}, G_OUT + t * 512, 512),
            sibling,
        )
        for t in range(2)
    ]
    for t in range(2):
        columns = slice(t * 512, (t + 1) * 512)
        grads_own(G_OUT + t * 512, 512, dot_tn(mixed[c], branch[:, :, columns].reshape(512, 512)))
    mixed_back = (
        dot_nt(all_branch(), weight_own(OUT0, 1024)).astype(BF16),
        dot_nt(all_branch(), weight_other(0, 1024)).astype(BF16),
    )
    for h, values in ((c, mixed_back[0]), (sib, mixed_back[1])):
        hidden_mid[h, :, 0:512] = values[:256]
        hidden_mid[h, :, 512:1024] = values[256:]
    arrive(to_sibling)
    reduce(3)
    exchange("mixed")
    gains_acc[2:3, :] = jnp.zeros((1, 1024), F32)

    def attend_back(step, carry):
        b, g = step // 4, step % 4
        rows, query, key, value = heads_of(b, g)
        column = lanes(b * 512 + g * 128, 128)
        pulled = jnp.concatenate([hidden_mid[h, :, column] for h in range(2)], axis=0)
        bias = mask_turned[b].astype(F32)
        scores = dot_nt(key, query) * (SCALE * LOG2E) + jnp.concatenate([bias, bias], axis=1)
        expo = jnp.exp2(scores)
        probs = expo * (1.0 / jnp.sum(expo, axis=0, keepdims=True))
        back_probs = dot_nt(value, pulled)
        inner = jnp.sum(probs * back_probs, axis=0, keepdims=True)
        back_scores = (probs * (back_probs - inner) * SCALE).astype(BF16)
        back_query = dot_tn(back_scores, key)
        back_key = dot(back_scores, query)
        back_value = dot(probs.astype(BF16), pulled)
        cosine = rope[b, :, 0:128]
        sine = rope[b, :, 128:256]

        def through(upstream, column, gain):
            values = raw[rows, lanes(column, 128)].astype(F32)
            scale = lax.rsqrt(head_mean(values * values) + EPS)
            unit = values * scale
            plain = upstream * cosine - pltpu.roll(upstream, 64, 1) * sine
            term = plain * unit
            pushed = plain * gain
            result = scale * (pushed - unit * head_mean(term * gain))
            gate_up[rows, lanes(column, 128)] = result.astype(BF16)
            return jnp.sum(term, axis=0, keepdims=True)

        for h in range(2):
            gains_acc[2:3, 0:128] += through(
                back_query[h * 256 : (h + 1) * 256], (2 * g + h) * 128, gain_query
            )
        gains_acc[2:3, 128:256] += through(back_key, 1024 + g * 128, gain_key)
        gate_up[rows, lanes(1536 + g * 128, 128)] = back_value.astype(BF16)
        return carry

    lax.fori_loop(0, 4, attend_back, 0)
    exchange("attend0")
    lax.fori_loop(4, 8, attend_back, 0)
    exchange("attend1")
    for transfer in to_sibling:
        transfer.sent()
        pending.remove(transfer)
    turned_lhs[...] = all_hidden().T.reshape(4, 4, 4, 16, 512)

    def qkv_grads(t, carry):
        values = dot(left(), gate_up[:, lanes(t * 256, 256)])
        column = t * 256 + jnp.where(t < 4, OUT0, DN0 - 1024)
        weights[:, :, :, :, lanes(column, 256)] = values.astype(BF16).reshape(4, 4, 4, 16, 256)
        return carry

    lax.fori_loop(0, 4, qkv_grads, 0)
    reduce(4)
    exchange("query")
    lax.fori_loop(4, 8, qkv_grads, 0)
    reduce(5)
    exchange("key")
    across_down.sent()
    pending.remove(across_down)

    def back_in(row, carry):
        values = dot_nt(gate_up[:, 0:2048], weight_rows(row, QKV0, 2048))
        two_parts(values, lanes(row * 256, 256))
        return carry

    lax.fori_loop(0, 4, back_in, 0)
    across = send(part.at[sib], got_part, got_part, sibling)
    across_down.arrived()
    hidden_mid[c] = (middle[...] + got_down[...]).astype(BF16)
    copy_out = pltpu.make_async_copy(hidden_mid.at[c], activations, local_sem.at[0])
    copy_out.start()
    exchange("in")
    arrive([across])
    back = part[c] + got_part[...]
    unit_in, scale_in = unit_of(toks[c].astype(F32))
    gains_acc[0:1, :] = jnp.sum(back * unit_in, axis=0, keepdims=True)
    back_middle = branch[c].astype(F32) + cots[c].astype(F32)
    hidden_mid[sib] = (back_middle + norm_back(back, gain_in, unit_in, scale_in)).astype(BF16)
    copy_in = pltpu.make_async_copy(hidden_mid.at[sib], input_grad, local_sem.at[1])
    copy_in.start()

    low = jnp.concatenate(
        [gains_acc[r : r + 1, i * 128 : (i + 1) * 128] for r in range(2) for i in range(8)], axis=0
    ).astype(BF16)
    high = jnp.concatenate(
        [gains_acc[2:3, 0:128], gains_acc[2:3, 128:256], jnp.zeros((14, 128), F32)], axis=0
    ).astype(BF16)
    gains_at = slice(DN0 + 1024, DN0 + 1152)
    weights[:, :, :, :, gains_at] = jnp.zeros((4, 4, 4, 16, 128), BF16)
    for part_x in range(4):
        for part_y in (0, 2):
            weights[part_x, part_y, 0, :, gains_at] = low
            weights[part_x, part_y, 1, :, gains_at] = high
    reduce(6)
    exchange("end")
    assert g_stage == [7] * UNITS, g_stage
    for unit in range(UNITS):
        arrive(sums[unit, 7])
    copy_out.wait()
    copy_in.wait()
    flush()
    assert used[0] <= TRANSFERS and local_count[0] <= 48, used


TRANSFERS = 416


def run_layer(*operands):
    anywhere = pl.BlockSpec(memory_space=pl.ANY)
    vmem = pltpu.VMEM
    return pl.pallas_call(
        layer_kernel,
        out_shape=(
            jax.ShapeDtypeStruct((TOK, D), BF16),
            jax.ShapeDtypeStruct((TOK, D), BF16),
            jax.ShapeDtypeStruct((2, 2, 4, 16, S_COLS), BF16),
        ),
        in_specs=[anywhere] * 9,
        out_specs=(anywhere,) * 3,
        scratch_shapes=[
            vmem((4, 4, 4, 16, WCOLS), BF16),
            vmem((4, 4, 4, 16, G_COLS), BF16),
            vmem((2, 4, 4, 16, 2560), BF16),
            vmem((2, 2, 4, 16, WCOLS), BF16),
            vmem((2, 4, 4, 16, WCOLS), BF16),
            vmem((3, 4, 16, WCOLS), BF16),
            vmem((3, 16, WCOLS), BF16),
            vmem((2, TOK, D), BF16),
            vmem((2, TOK, D), BF16),
            vmem((2, TOK, 256), F32),
            vmem((2, TOK, TOK), BF16),
            vmem((2, TOK, TOK), BF16),
            vmem((2, TOK, D), BF16),
            vmem((2 * TOK, 1536), BF16),
            vmem((12, 2 * TOK, HD), BF16),
            vmem((4, 2 * TOK, HD), BF16),
            vmem((2, 2 * TOK, 512), BF16),
            vmem((2, TOK, D), F32),
            vmem((TOK, D), F32),
            vmem((TOK, D), F32),
            vmem((TOK, D), F32),
            vmem((2, TOK, D), BF16),
            vmem((2 * TOK, 3072), BF16),
            vmem((3, 2 * TOK, 512), BF16),
            vmem((2, TOK, D), BF16),
            vmem((4, 4, 4, 16, 2 * TOK), BF16),
            vmem((2, 4, 4, 16, 2 * TOK), BF16),
            vmem((8, D), F32),
            pltpu.SemaphoreType.DMA((48,)),
            pltpu.SemaphoreType.DMA((TRANSFERS,)),
            pltpu.SemaphoreType.DMA((TRANSFERS,)),
        ],
        compiler_params=pltpu.CompilerParams(
            collective_id=0, has_side_effects=True, vmem_limit_bytes=64 * 2**20
        ),
        cost_estimate=pl.CostEstimate(flops=26 * 10**9, bytes_accessed=10**7, transcendentals=10**6),
    )(*operands)


def adamw(master, first, second, gradient, rate, decay):
    first_new = 0.9 * first + 0.1 * gradient
    second_new = 0.999 * second + 0.001 * gradient * gradient
    direction = first_new / (1.0 - 0.9**STEP) / (jnp.sqrt(second_new / (1.0 - 0.999**STEP)) + 1e-08)
    return (master - rate * (direction + decay * master), first_new, second_new)


def step_places():
    qkv = [(0, c * 1024, c, S_QKV, 1024) for c in range(2)]
    qkv += [(0, 2048 + c * 512, c, S_QKV + 1024, 512) for c in range(2)]
    qkv += [(0, 3072 + c * 512, c, S_QKV + 1536, 512) for c in range(2)]
    out = [(c, 0, c, S_OUT, 1024) for c in range(2)]
    gate_up = [
        (0, up * 3072 + c * 1536 + half * 768, c, S_GU + half * 1536 + up * 768, 768)
        for up in range(2)
        for c in range(2)
        for half in range(2)
    ]
    down = [(0, 0, 0, S_DN, 1024), (2, 0, 1, S_DN, 1024)]
    down += [(1, c * 512, c, S_DN + 1024, 512) for c in range(2)]
    return qkv, out, gate_up, down


def step_kernel(*refs):
    states, summed, news = refs[:12], refs[12], refs[13:]
    for index, places in enumerate(step_places()):
        master, first, second = states[3 * index : 3 * index + 3]
        for group, column, core, at, size in places:
            here = (group, slice(None), pl.ds(column, size))
            results = adamw(
                master[here],
                first[here],
                second[here],
                summed[core, :, pl.ds(at, size)].astype(F32),
                0.05,
                0.1,
            )
            for ref, value in zip(news[3 * index : 3 * index + 3], results):
                ref[here] = value


def step(masters, firsts, seconds, summed):
    rows = 16
    arrays, specs, shapes = [], [], []
    for state in zip(masters, firsts, seconds):
        for array in state:
            groups = array.shape[0] // 128
            arrays.append(array.reshape(groups, 128, -1))
            specs.append(pl.BlockSpec((groups, rows, array.shape[1]), lambda i: (0, i, 0)))
            shapes.append(jax.ShapeDtypeStruct(arrays[-1].shape, F32))
    results = pl.pallas_call(
        step_kernel,
        grid=(128 // rows,),
        out_shape=tuple(shapes),
        in_specs=specs + [pl.BlockSpec((2, rows, S_COLS), lambda i: (0, i, 0))],
        out_specs=tuple(specs),
        compiler_params=pltpu.CompilerParams(vmem_limit_bytes=62 * 2**20),
        cost_estimate=pl.CostEstimate(flops=3 * 10**7, bytes_accessed=5 * 10**7, transcendentals=10**6),
    )(*arrays, summed)
    results = [value.reshape(-1, value.shape[2]) for value in results]
    return [tuple(results[3 * index : 3 * index + 3]) for index in range(4)]


def per_device(
    tokens,
    cotangent,
    segment_ids,
    positions,
    master_qkv,
    master_out,
    master_gate_up,
    master_down,
    master_gains,
    first_qkv,
    first_out,
    first_gate_up,
    first_down,
    first_gains,
    second_qkv,
    second_out,
    second_gate_up,
    second_down,
    second_gains,
):
    me = coordinates()
    shard = lax.axis_index("shard")
    order = jnp.minimum((me["y"] % 2) * 4 + me["z"], 2)
    gains = lax.dynamic_slice(
        jnp.pad(master_gains, (2048, 6144)), (2048 + 2048 * order - 288 * shard,), (2048,)
    ).reshape(16, 128)

    freq = jnp.exp(jnp.arange(HD // 2).astype(F32) * (-2.0 * math.log(1000000.0) / HD))
    angle = positions[0].astype(F32)[:, None] * freq
    cosine = jnp.cos(angle)
    sine = jnp.sin(angle)
    tables = jnp.concatenate([cosine, sine], axis=-1)

    activations, input_grad, summed = run_layer(
        tokens,
        cotangent,
        tables,
        jnp.broadcast_to(segment_ids.astype(F32), (8, TOK)),
        gains,
        master_qkv,
        master_out,
        master_gate_up,
        master_down,
    )
    summed = summed.reshape(2, 128, S_COLS)
    gain_rows = summed[:, :32, S_GAIN : S_GAIN + 128].astype(F32).sum(axis=0).reshape(-1)
    grad_gains = lax.dynamic_slice(gain_rows, (288 * shard,), (288,))
    updated = step(
        (master_qkv, master_out, master_gate_up, master_down),
        (first_qkv, first_out, first_gate_up, first_down),
        (second_qkv, second_out, second_gate_up, second_down),
        summed,
    )
    updated.append(adamw(master_gains, first_gains, second_gains, grad_gains, 0.4, 0.0))
    return (
        activations,
        input_grad,
        *(new[0] for new in updated),
        *(new[1] for new in updated),
        *(new[2] for new in updated),
    )


def solution(mesh):
    rows = P(("rep", "shard"), None)
    state = (P("shard", None),) * 4 + (P("shard"),)
    return jax.shard_map(
        per_device,
        mesh=mesh,
        in_specs=(rows,) * 4 + state * 3,
        out_specs=(rows,) * 2 + state * 3,
        check_vma=False,
    )
```

time: 246 us -> 202 us (0.82)
  local copies, waits for them, and re-layouts: 19.1 us -> 3.55 us
  other arithmetic: 18.2 us -> 4.78 us
  Pallas kernels: 206 us -> 193 us
    pallas_call x1, Pallas kernels: 206 us -> 174 us  [run_layer(): pl.pallas_call(layer_kernel, out_shape=(jax.ShapeDtypeStruct((TOK, D), BF...]
    pallas_call x0 -> x1, Pallas kernels: none -> 18.9 us  [step(): pl.pallas_call(step_kernel, grid=(128 // rows,), out_shape=tuple(shapes),...]
    sub x5 -> x1, other arithmetic: 14.4 us -> 1.39 us  [adamw(): return (master - rate * (direction + decay * master), first_new, second_new)]
    unnamed x47 -> x6, local copies, waits for them, and re-layouts: 13.8 us -> 1.6 us
    slice x7 -> x0, local copies, waits for them, and re-layouts: 3.63 us -> none  [the longest x1 2.84 us: per_device(): g0, g1 = (gradient[0], gradient[1])]
where the time goes in v2:
time: 202 us
  Pallas kernels  193 us (96%)
  other arithmetic  4.78 us (2%)
  local copies, waits for them, and re-layouts  3.55 us (2%)
    pallas_call x1, Pallas kernels, run_layer(): pl.pallas_call(layer_kernel, out_shape=(jax.ShapeDtypeStruct((TOK, D), BF...  174 us
    pallas_call x1, Pallas kernels, step(): pl.pallas_call(step_kernel, grid=(128 // rows,), out_shape=tuple(shapes),...  18.9 us

profile of v2, /device:TPU:1, one launch (start us, length us, event | category | flops | bytes accessed | tf_op | source)
XLA Modules:
  0.0 202.0 jit_solution(3812402453270456413)
XLA Ops:
  0.7 0.7 convert_element_type.28
  1.4 0.7 convert_element_type.25
  2.1 0.6 broadcast_in_dim.10.segments
  2.7 1.4 fusion.gains
  4.1 0.5 multiply_cosine_fusion
  4.6 0.8 pad_maximum_fusion.tables
  5.4 174.0 %shard_map.314 = (bf16[256,1024]{1,0:T(8,128)(2,1)}, bf16[256,1024]{1,0:T(8,128)(2,1)}, bf16[2,2,4,16,8192]{4,3,2,1,0:T(8,128)(2,1)}) custom-call(bf16[256,1024]{1,0:T(8,128)(2,1)} %tokens.1, bf16[256,1024]{1,0:T(8,128)(2,1)} %cotangent.1, f32[256,128]{1,0:T(8,128)} %pad_maximum_fusion.tables, f32[8,256]{1,0:T(8,128)} %broadcast_in_dim.10.segments, ...), custom_call_target="tpu_custom_call" | custom-call | flops 25999998976 | bytes 10000000 | tf_op jit(solution)/shard_map/pallas_call | solution.py:979
  179.4 0.7 convert_reduce_fusion
  180.1 1.4 multiply_subtract_fusion
  181.5 0.0 copy-start.1
  181.5 0.0 copy-start
  181.5 18.9 %shard_map.315 = (f32[1,128,4096]{2,1,0:T(8,128)}, f32[1,128,4096]{2,1,0:T(8,128)}, f32[1,128,4096]{2,1,0:T(8,128)}, f32[2,128,1024]{2,1,0:T(8,128)}, f32[2,128,...) custom-call(f32[1,128,4096]{2,1,0:T(8,128)} %bitcast.35, ...), custom_call_target="tpu_custom_call" | custom-call | flops 30000000 | bytes 50000000 | tf_op jit(solution)/shard_map/pallas_call | solution.py:1078
  200.4 0.0 copy-done.1
  200.4 0.8 copy.38
  201.2 0.0 copy-done
  201.2 0.8 copy.39
  (1 shorter events, 0.0 us)
Async XLA Ops:
  181.5 18.9 %copy-start.1 = (bf16[256,1024]{1,0:T(8,128)(2,1)S(1)}, bf16[256,1024]{1,0:T(8,128)(2,1)}, u32[]{:S(2)}) copy-start(bf16[256,1024]{1,0:T(8,128)(2,1)} %get-tuple-element.69) | copy-start | bytes 1572868
  181.5 19.7 %copy-start = (bf16[256,1024]{1,0:T(8,128)(2,1)S(1)}, bf16[256,1024]{1,0:T(8,128)(2,1)}, u32[]{:S(2)}) copy-start(bf16[256,1024]{1,0:T(8,128)(2,1)} %get-tuple-element.70) | copy-start | bytes 1572868
